TPU v7x, 128 devices: a whole 4x4x4 slice. The times are simulated.
128 devices in a mesh: gx: 16 (over x, z), gy: 8 (over y, core).
Axes of the slice: x: 4, y: 4, z: 4, core: 2. Of those that a mesh axis runs over, the one named last changes fastest.
Arguments:
- tokens: bfloat16 [3, 256, 18432], P(None, 'gy', 'gx'), may hold values from -6 to 6
- q_weight: bfloat16 [18432, 12288], P('gx', 'gy'), may hold values from -0.046875 to 0.046875
- kv_weight: bfloat16 [18432, 512], P('gx'), may hold values from -0.046875 to 0.046875
- out_weight: bfloat16 [12288, 18432], P('gy', 'gx'), may hold values from -0.0546875 to 0.0546875
- kv_cache: bfloat16 [256, 8192, 512], P(('gx', 'gy')), may hold values from -92 to 92, as said below
- lengths: int32 [256], P(('gx', 'gy')), may hold values from 1024 to 8189, as said below
Outputs:
- attn_out: bfloat16 [3, 256, 18432], P(None, 'gy', 'gx')
Inputs may be any that keep to these rules, and one draw needn't show every extreme that they name: Request r's tokens of step s sit at cache slot lengths[r] + s; some request has the most and some the fewest. `kv_cache`: slots at and beyond a request's length hold stale entries.
All inputs are finite; a program needn't handle non-finite values.
Results may differ from a plain program's by a relative error of at most 0.035.
Values may be sent and summed in bfloat16 or wider, within the bound.
No kernel may reach another device: no remote copies, remote signals or barrier semaphores. Data moves between devices by JAX's collectives and lax.ppermute only.
A program may use at most 256 MiB of HBM per device.

v0:
```python
import jax
import jax.numpy as jnp
from jax import lax
from jax.sharding import PartitionSpec as P

STEPS = 3


def rotate(values, positions):
    head_dim = values.shape[-1]
    half_dim = head_dim // 2
    frequency = 10000.0 ** (-(jnp.arange(half_dim, dtype=jnp.float32) * 2.0 / head_dim))
    angles = positions[..., None] * frequency
    cosine = jnp.cos(angles)
    sine = jnp.sin(angles)
    front_half = values[..., :half_dim]
    back_half = values[..., half_dim:]
    return jnp.concatenate(
        [front_half * cosine - back_half * sine, back_half * cosine + front_half * sine], -1
    )


def place_rows(store, new_rows, slot):
    return lax.dynamic_update_slice(store, new_rows, (slot, jnp.int32(0)))


def attend_blocks(queries, store, limits, block_count, block_size):
    req_local, query_rows, head_dim = queries.shape

    def one_block(block_index, state_tuple):
        running_max, denom, accum = state_tuple
        piece = lax.dynamic_slice_in_dim(store, block_index * block_size, block_size, 1)
        keys = piece[:, :, :head_dim]
        values = piece[:, :, head_dim:]
        scores = (
            jnp.einsum("rhd,rkd->rhk", queries, keys, preferred_element_type=jnp.float32) / 16.0
        )
        slot_ids = block_index * block_size + jnp.arange(block_size, dtype=jnp.int32)
        visible = slot_ids[None, None, :] <= limits[:, :, None]
        scores = jnp.where(visible, scores, jnp.float32(-1e30))
        new_max = jnp.maximum(running_max, jnp.max(scores, axis=-1))
        weights = jnp.where(visible, jnp.exp(scores - new_max[..., None]), jnp.float32(0.0))
        factor = jnp.exp(running_max - new_max)
        denom = denom * factor + jnp.sum(weights, axis=-1)
        mixed = jnp.einsum(
            "rhk,rkd->rhd", weights.astype(jnp.bfloat16), values, preferred_element_type=jnp.float32
        )
        accum = accum * factor[..., None] + mixed
        return (new_max, denom, accum)

    start_state = (
        jnp.full((req_local, query_rows), -1e30, jnp.float32),
        jnp.zeros((req_local, query_rows), jnp.float32),
        jnp.zeros((req_local, query_rows, head_dim), jnp.float32),
    )
    running_max, denom, accum = lax.fori_loop(0, block_count, one_block, start_state)
    return (accum / denom[..., None]).astype(jnp.bfloat16)


def per_device(tokens, q_weight, kv_weight, out_weight, kv_cache, lengths):
    gy_count = lax.axis_size("gy")
    gy_index = lax.axis_index("gy")
    req_local = kv_cache.shape[0]
    slot_total = kv_cache.shape[1]
    head_dim = kv_cache.shape[2] // 2
    query_cols = q_weight.shape[1]
    heads_local = query_cols // head_dim
    heads_all = heads_local * gy_count
    block_size = min(1024, slot_total)
    block_rows = req_local * gy_count
    joined_weights = jnp.concatenate([q_weight, kv_weight], 1)
    groups = [(step_index, step_index + 1) for step_index in range(STEPS)]
    store_all = kv_cache
    results = []
    for first_step, end_step in groups:
        count = end_step - first_step
        step_tokens = jnp.transpose(tokens[first_step:end_step], (1, 0, 2))
        gathered = lax.all_gather(step_tokens, "gy", axis=0, tiled=True)
        offsets = jnp.arange(first_step, end_step, dtype=jnp.int32)
        slots = lengths[:, None] + offsets[None, :]
        summed = lax.psum_scatter(
            jnp.einsum(
                "rsd,dc->rsc", gathered, joined_weights, preferred_element_type=jnp.float32
            ).astype(jnp.bfloat16),
            "gx",
            scatter_dimension=0,
            tiled=True,
        ).astype(jnp.float32)
        query_linear = (
            summed[..., :query_cols]
            .astype(jnp.bfloat16)
            .reshape(block_rows, count, heads_local, head_dim)
        )
        query_mine = lax.all_to_all(query_linear, "gy", split_axis=0, concat_axis=2, tiled=True)
        own_rows = lax.dynamic_slice_in_dim(summed, gy_index * req_local, req_local, 0)
        kv_rows = own_rows[..., query_cols:].astype(jnp.bfloat16)
        pos_float = slots.astype(jnp.float32)
        queries = rotate(query_mine.astype(jnp.float32), pos_float[:, :, None]).astype(jnp.bfloat16)
        new_keys = rotate(kv_rows[..., :head_dim].astype(jnp.float32), pos_float).astype(
            jnp.bfloat16
        )
        new_rows = jnp.concatenate([new_keys, kv_rows[..., head_dim:]], -1)
        store_all = jax.vmap(place_rows)(store_all, new_rows, slots[:, 0])
        flat_queries = queries.reshape(req_local, count * heads_all, head_dim)
        limits = jnp.broadcast_to(slots[:, :, None], (req_local, count, heads_all)).reshape(
            req_local, count * heads_all
        )
        block_count = slot_total // block_size
        attended = attend_blocks(flat_queries, store_all, limits, block_count, block_size)
        attended = attended.reshape(req_local, count, heads_all, head_dim)
        returned = lax.all_to_all(attended, "gy", split_axis=2, concat_axis=0, tiled=True)
        returned = returned.reshape(block_rows, count, query_cols)
        all_rows = lax.all_gather(returned, "gx", axis=0, tiled=True)
        out_rows = lax.psum_scatter(
            jnp.einsum(
                "rsh,hd->rsd", all_rows, out_weight, preferred_element_type=jnp.float32
            ).astype(jnp.bfloat16),
            "gy",
            scatter_dimension=0,
            tiled=True,
        )
        results.append(jnp.transpose(out_rows, (1, 0, 2)))
    return jnp.concatenate(results, 0)


def solution(mesh):
    in_specs = (
        P(None, "gy", "gx"),
        P("gx", "gy"),
        P("gx", None),
        P("gy", "gx"),
        P(("gx", "gy"), None, None),
        P(("gx", "gy")),
    )
    out_specs = P(None, "gy", "gx")
    return jax.shard_map(
        per_device, mesh=mesh, in_specs=in_specs, out_specs=out_specs, check_vma=False
    )
```

profile of v0, /device:TPU:0, one launch (start us, length us, event | category | flops | bytes accessed | tf_op | source)
XLA Modules:
  0.0 626.2 jit_solution(6772569599568539796)
XLA Ops:
  6.5 14.7 %copy.225 = bf16[2,8192,512]{2,1,0:T(8,128)(2,1)} copy(bf16[2,8192,512]{2,1,0:T(8,128)(2,1)} %param.16) | data formatting | bytes 33554432
  21.3 13.9 %all-gather.2 = bf16[1,256,1152]{2,1,0:T(8,128)(2,1)S(1)} all-gather(bf16[1,32,1152]{2,1,0:T(8,128)(2,1)S(1)} %get-tuple-element.725), channel_id=4, replica_groups=mesh['gx'=16,'gy'=8] {'gy'}, dimensions={1}, use_global_device_ids=true | all-gather | bytes 663552 | tf_op jit(solution)/shard_map/all_gather | solution.py:78
  35.2 13.2 %all-gather = bf16[1,256,1152]{2,1,0:T(8,128)(2,1)S(1)} all-gather(bf16[1,32,1152]{2,1,0:T(8,128)(2,1)S(1)} %get-tuple-element.726), channel_id=2, replica_groups=mesh['gx'=16,'gy'=8] {'gy'}, dimensions={1}, use_global_device_ids=true | all-gather | bytes 663552 | tf_op jit(solution)/shard_map/all_gather | solution.py:78
  48.3 13.2 %all-gather.1 = bf16[1,256,1152]{2,1,0:T(8,128)(2,1)S(1)} all-gather(bf16[1,32,1152]{2,1,0:T(8,128)(2,1)S(1)} %get-tuple-element.727), channel_id=3, replica_groups=mesh['gx'=16,'gy'=8] {'gy'}, dimensions={1}, use_global_device_ids=true | all-gather | bytes 663552 | tf_op jit(solution)/shard_map/all_gather | solution.py:78
  62.2 2.7 fusion.56
  64.9 2.6 fusion.55
  67.5 2.6 fusion.54
  70.1 6.0 copy.109
  76.2 6.0 copy.119
  82.2 6.1 copy.129
  96.7 116.3 %all-reduce.9.cloned.1.call-done = (bf16[256,1,2048]{2,1,0:T(2,128)(2,1)}, bf16[256,1,2048]{2,1,0:T(2,128)(2,1)}, bf16[256,1,2048]{2,1,0:T(2,128)(2,1)}) async-done(((bf16[256,1,2048]{2,1,0:T(2,128)(2,1)}, bf16[256,1,2048]{2,1,0:T(2,128)(2,1)}, bf16[256,1,2048]{2,1,0:T(2,128)(2,1)}), (bf16[256,1,2048]{2,1,0:T(2,128)(2,1)}, bf16[256,1,2048]{2,1,0:T(2,128)(2,1)}, ...) | async-done | bytes 3145744
  217.9 4.3 all-to-all-start
  227.3 19.6 %while.57 = (s32[]{:T(128)}, bf16[2,8192,512]{2,1,0:T(8,128)(2,1)}, s32[2,3]{1,0:T(2,128)}, bf16[2,1,512]{2,0,1:T(2,128)(2,1)}, s32[]{:T(128)}, /*index=5*/s32[3]{0:T(128)}, s32[]{:T(128)}) while((s32[]{:T(128)}, bf16[2,8192,512]{2,1,0:T(8,128)(2,1)}, s32[2,3]{1,0:T(2,128)}, bf16[2,1,512]{2,0,1:T(2,128)(2,1)}, s32[]{:T(128)}, /*index=5*/s32[3]{0:T(128)}, ...), condition=%wide.while_cond, body=%wide.while_body.sunk | while | flops 531 | bytes 5299 | solution.py:24
  228.7 3.3 and_reduce_fusion.6
  232.0 2.6 broadcast_select_fusion.9
  238.5 3.3 and_reduce_fusion.6
  241.8 2.6 broadcast_select_fusion.9
  244.4 2.5 dynamic-update-slice.13
  246.9 13.8 %copy.177 = bf16[2,8192,512]{2,1,0:T(8,128)(2,1)} copy(bf16[2,8192,512]{2,1,0:T(8,128)(2,1)} %get-tuple-element.1163) | data formatting | bytes 33554432
  261.3 19.6 %while.58 = (s32[]{:T(128)}, bf16[2,8192,512]{2,1,0:T(8,128)(2,1)}, s32[2,3]{1,0:T(2,128)}, bf16[2,1,512]{2,0,1:T(2,128)(2,1)}, s32[]{:T(128)}, /*index=5*/s32[3]{0:T(128)}, s32[]{:T(128)}) while((s32[]{:T(128)}, bf16[2,8192,512]{2,1,0:T(8,128)(2,1)}, s32[2,3]{1,0:T(2,128)}, bf16[2,1,512]{2,0,1:T(2,128)(2,1)}, s32[]{:T(128)}, ...), condition=%wide.while_cond.1, body=%wide.while_body.1.sunk | while | flops 531 | bytes 5299 | solution.py:24
  262.6 3.3 and_reduce_fusion.7
  265.9 2.6 broadcast_select_fusion.10
  268.5 2.6 dynamic-update-slice.14
  272.4 3.3 and_reduce_fusion.7
  275.7 2.6 broadcast_select_fusion.10
  278.3 2.6 dynamic-update-slice.14
  280.9 13.8 %copy.183 = bf16[2,8192,512]{2,1,0:T(8,128)(2,1)} copy(bf16[2,8192,512]{2,1,0:T(8,128)(2,1)} %get-tuple-element.1127) | data formatting | bytes 33554432
  295.3 19.9 %while.59 = (s32[]{:T(128)}, bf16[2,8192,512]{2,1,0:T(8,128)(2,1)}, s32[2,3]{1,0:T(2,128)}, bf16[2,1,512]{2,0,1:T(2,128)(2,1)}, s32[]{:T(128)}, /*index=5*/s32[3]{0:T(128)}, s32[]{:T(128)}) while((s32[]{:T(128)}, bf16[2,8192,512]{2,1,0:T(8,128)(2,1)}, s32[2,3]{1,0:T(2,128)}, bf16[2,1,512]{2,0,1:T(2,128)(2,1)}, s32[]{:T(128)}, ...), condition=%wide.while_cond.2, body=%wide.while_body.2.sunk | while | flops 531 | bytes 5299 | solution.py:24
  296.5 3.4 and_reduce_fusion.8
  299.9 2.6 broadcast_select_fusion.11
  302.6 2.6 dynamic-update-slice.15
  306.5 3.4 and_reduce_fusion.8
  309.9 2.6 broadcast_select_fusion.11
  312.5 2.6 dynamic-update-slice.15
  320.1 4.8 all-to-all-start.2
  333.8 52.1 %while.60 = (s32[]{:T(128)}, f32[2,48]{1,0:T(2,128)}, f32[2,48]{1,0:T(2,128)}, f32[2,48,256]{2,1,0:T(8,128)}, bf16[2,8192,512]{2,1,0:T(8,128)(2,1)}, /*index=5*/...) while((s32[]{:T(128)}, f32[2,48]{1,0:T(2,128)}, ...), condition=%wide.region_5.6_spmd.clone, body=%wide.region_2.5_spmd.clone.sunk | while | flops 101918176 | bytes 3545323 | solution.py:56
  388.9 4.0 all-to-all-start.1
  394.5 4.0 all-to-all-done.1
  398.4 4.0 all-to-all-start.4
  405.4 23.9 %all_gather.19 = bf16[256,1,1536]{2,0,1:T(8,128)(2,1)S(1)} all-gather(bf16[16,1,1536]{2,0,1:T(8,128)(2,1)} %reshape.731), channel_id=1, replica_groups=mesh['gx'=16,'gy'=8] {'gx'}, dimensions={0}, use_global_device_ids=true | all-gather | bytes 835584 | tf_op jit(solution)/shard_map/all_gather | solution.py:113
  431.5 42.9 %while.61 = (s32[]{:T(128)}, f32[2,48]{1,0:T(2,128)S(1)}, f32[2,48]{1,0:T(2,128)}, f32[2,48,256]{2,1,0:T(8,128)}, bf16[2,8192,512]{2,1,0:T(8,128)(2,1)}, /*index...) while((s32[]{:T(128)}, f32[2,48]{1,0:T(2,128)S(1)}, ...), condition=%wide.region_12.13_spmd.clone, body=%wide.region_9.12_spmd.clone.sunk | while | flops 101918176 | bytes 3545323 | solution.py:56
  480.5 4.6 all-to-all-start.3
  486.8 4.0 all-to-all-done.3
  493.8 22.4 %all_gather.21 = bf16[256,1,1536]{2,0,1:T(8,128)(2,1)S(1)} all-gather(bf16[16,1,1536]{2,0,1:T(8,128)(2,1)} %reshape.736), channel_id=1, replica_groups=mesh['gx'=16,'gy'=8] {'gx'}, dimensions={0}, use_global_device_ids=true | all-gather | bytes 835584 | tf_op jit(solution)/shard_map/all_gather | solution.py:113
  518.4 34.4 %while.62 = (s32[]{:T(128)}, f32[2,48]{1,0:T(2,128)S(1)}, f32[2,48]{1,0:T(2,128)S(1)}, f32[2,48,256]{2,1,0:T(8,128)}, bf16[2,8192,512]{2,1,0:T(8,128)(2,1)}, /*i...) while((s32[]{:T(128)}, f32[2,48]{1,0:T(2,128)S(1)}, ...), condition=%wide.region_19.20_spmd.clone, body=%wide.region_16.19_spmd.clone.sunk | while | flops 101918176 | bytes 3545323 | solution.py:56
  554.5 7.9 %all_to_all.72 = bf16[2,1,48,256]{3,0,1,2:T(2,128)(2,1)S(1)} all-to-all(bf16[2,1,48,256]{3,0,1,2:T(2,128)(2,1)S(1)} %fusion.69), channel_id=1, replica_groups=mesh['gx'=16,'gy'=8] {'gy'}, dimensions={2} | all-to-all | bytes 98304 | tf_op jit(solution)/shard_map/all_to_all | solution.py:111
  564.6 23.2 %all_gather.23 = bf16[256,1,1536]{2,0,1:T(8,128)(2,1)S(1)} all-gather(bf16[16,1,1536]{2,0,1:T(8,128)(2,1)} %reshape.741), channel_id=1, replica_groups=mesh['gx'=16,'gy'=8] {'gx'}, dimensions={0}, use_global_device_ids=true | all-gather | bytes 835584 | tf_op jit(solution)/shard_map/all_gather | solution.py:113
  589.9 28.1 %reduce-scatter.8.cloned.1.call-done = bf16[32,1,1152]{2,0,1:T(8,128)(2,1)} async-done(((bf16[256,1,1152]{2,0,1:T(8,128)(2,1)}), bf16[32,1,1152]{2,0,1:T(8,128)(2,1)}) %reduce-scatter.8.cloned.1.call-update) | async-done | bytes 73744 | tf_op jit(solution)/shard_map/reduce_scatter | solution.py:114
  (299 shorter events, 203.3 us)
Async XLA Ops:
  6.5 422.8 %copy-start = (bf16[1536,1152]{1,0:T(8,128)(2,1)S(1)}, bf16[1536,1152]{1,0:T(8,128)(2,1)}, u32[]{:S(2)}) copy-start(bf16[1536,1152]{1,0:T(8,128)(2,1)} %param.15) | copy-start | bytes 10616836
  6.5 206.4 %all-reduce.9.cloned.1.call-start = ((), (), s32[]{:S(2)}) async-start(), calls=%async_computation.12 | async-start | bytes 12582912
  6.5 14.7 %copy-start.3 = (bf16[3,32,1152]{2,1,0:T(8,128)(2,1)S(1)}, bf16[3,32,1152]{2,1,0:T(8,128)(2,1)}, u32[]{:S(2)}) copy-start(bf16[3,32,1152]{2,1,0:T(8,128)(2,1)} %param.12) | copy-start | bytes 663556
  6.5 55.0 %copy-start.1 = (bf16[1152,1536]{1,0:T(8,128)(2,1)S(1)}, bf16[1152,1536]{1,0:T(8,128)(2,1)}, u32[]{:S(2)}) copy-start(bf16[1152,1536]{1,0:T(8,128)(2,1)} %param.13) | copy-start | bytes 10616836
  21.2 40.8 %copy-start.2 = (bf16[1152,512]{1,0:T(8,128)(2,1)S(1)}, bf16[1152,512]{1,0:T(8,128)(2,1)}, u32[]{:S(2)}) copy-start(bf16[1152,512]{1,0:T(8,128)(2,1)} %param.14) | copy-start | bytes 3538948
  82.2 6.2 copy-start.4
  82.2 6.8 %copy-start.15 = (s32[2]{0:T(128)S(1)}, s32[2]{0:T(128)}, u32[]{:S(2)}) copy-start(s32[2]{0:T(128)} %constant.187.clone.1) | copy-start | bytes 28
  94.8 0.5 copy-start.10
  217.9 102.2 %all-to-all-start = ((bf16[16,1,6,256]{3,2,1,0:T(8,128)(2,1)}), bf16[16,1,6,256]{3,2,1,0:T(8,128)(2,1)}, u32[]{:S(2)}, u32[]{:S(2)}) async-start(bf16[16,1,6,256]{3,2,1,0:T(8,128)(2,1)} %bitcast.179), calls=%async_computation | async-start | bytes 131072 | tf_op jit(solution)/shard_map/all_to_all | solution.py:94
  246.9 13.8 %copy-start.9 = (bf16[2,1,256]{2,0,1:T(2,128)(2,1)S(1)}, bf16[2,1,256]{2,0,1:T(2,128)(2,1)}, u32[]{:S(2)}) copy-start(bf16[2,1,256]{2,0,1:T(2,128)(2,1)} %get-tuple-element.737) | copy-start | bytes 3076
  246.9 13.8 %copy-start.13 = (bf16[2,1,128]{2,0,1:T(2,128)(2,1)S(1)}, bf16[2,1,128]{2,0,1:T(2,128)(2,1)}, u32[]{:S(2)}) copy-start(bf16[2,1,128]{2,0,1:T(2,128)(2,1)} %get-tuple-element.764) | copy-start | bytes 1540
  246.9 13.8 %copy-start.14 = (bf16[2,1,128]{2,0,1:T(2,128)(2,1)S(1)}, bf16[2,1,128]{2,0,1:T(2,128)(2,1)}, u32[]{:S(2)}) copy-start(bf16[2,1,128]{2,0,1:T(2,128)(2,1)} %get-tuple-element.765) | copy-start | bytes 1540
  280.9 13.8 %copy-start.8 = (bf16[2,1,256]{2,0,1:T(2,128)(2,1)S(1)}, bf16[2,1,256]{2,0,1:T(2,128)(2,1)}, u32[]{:S(2)}) copy-start(bf16[2,1,256]{2,0,1:T(2,128)(2,1)} %get-tuple-element.735) | copy-start | bytes 3076
  280.9 13.8 %copy-start.11 = (bf16[2,1,128]{2,0,1:T(2,128)(2,1)S(1)}, bf16[2,1,128]{2,0,1:T(2,128)(2,1)}, u32[]{:S(2)}) copy-start(bf16[2,1,128]{2,0,1:T(2,128)(2,1)} %get-tuple-element.740) | copy-start | bytes 1540
  280.9 13.8 %copy-start.12 = (bf16[2,1,128]{2,0,1:T(2,128)(2,1)S(1)}, bf16[2,1,128]{2,0,1:T(2,128)(2,1)}, u32[]{:S(2)}) copy-start(bf16[2,1,128]{2,0,1:T(2,128)(2,1)} %get-tuple-element.741) | copy-start | bytes 1540
  320.1 10.5 %all-to-all-start.2 = ((bf16[16,1,6,256]{3,2,1,0:T(8,128)(2,1)}), bf16[16,1,6,256]{3,2,1,0:T(8,128)(2,1)}, u32[]{:S(2)}, u32[]{:S(2)}) async-start(bf16[16,1,6,256]{3,2,1,0:T(8,128)(2,1)} %bitcast.180), calls=%async_computation.3 | async-start | bytes 131072 | tf_op jit(solution)/shard_map/all_to_all | solution.py:94
  385.9 45.5 %copy-start.6 = (f32[2,48]{1,0:T(2,128)S(1)}, f32[2,48]{1,0:T(2,128)}, u32[]{:S(2)}) copy-start(f32[2,48]{1,0:T(2,128)} %custom-call.3) | copy-start | bytes 1156
  388.9 9.5 %all-to-all-start.1 = ((bf16[2,1,48,256]{3,0,1,2:T(2,128)(2,1)}), bf16[2,1,48,256]{3,0,1,2:T(2,128)(2,1)}, u32[]{:S(2)}, u32[]{:S(2)}) async-start(bf16[2,1,48,256]{3,0,1,2:T(2,128)(2,1)} %fusion.71), calls=%async_computation.1 | async-start | bytes 98304 | tf_op jit(solution)/shard_map/all_to_all | solution.py:111
  398.4 76.0 %all-to-all-start.4 = ((bf16[16,1,6,256]{3,2,1,0:T(8,128)(2,1)}), bf16[16,1,6,256]{3,2,1,0:T(8,128)(2,1)}, u32[]{:S(2)}, u32[]{:S(2)}) async-start(bf16[16,1,6,256]{3,2,1,0:T(8,128)(2,1)} %bitcast.178), calls=%async_computation.6 | async-start | bytes 131072 | tf_op jit(solution)/shard_map/all_to_all | solution.py:94
  402.4 187.5 %reduce-scatter.4.cloned.1.call-start = ((), (), s32[]{:S(2)}) async-start(), calls=%async_computation.9 | async-start | bytes 663552 | tf_op jit(solution)/shard_map/reduce_scatter | solution.py:114
  474.4 44.0 %copy-start.5 = (f32[2,48]{1,0:T(2,128)S(1)}, f32[2,48]{1,0:T(2,128)}, u32[]{:S(2)}) copy-start(f32[2,48]{1,0:T(2,128)} %custom-call.6) | copy-start | bytes 1156
  474.4 44.0 %copy-start.7 = (f32[2,48]{1,0:T(2,128)S(1)}, f32[2,48]{1,0:T(2,128)}, u32[]{:S(2)}) copy-start(f32[2,48]{1,0:T(2,128)} %custom-call.7) | copy-start | bytes 1156
  480.5 10.3 %all-to-all-start.3 = ((bf16[2,1,48,256]{3,0,1,2:T(2,128)(2,1)}), bf16[2,1,48,256]{3,0,1,2:T(2,128)(2,1)}, u32[]{:S(2)}, u32[]{:S(2)}) async-start(bf16[2,1,48,256]{3,0,1,2:T(2,128)(2,1)} %fusion.70), calls=%async_computation.4 | async-start | bytes 98304 | tf_op jit(solution)/shard_map/all_to_all | solution.py:111
  485.2 104.7 %reduce-scatter.6.cloned.1.call-start = ((), (), s32[]{:S(2)}) async-start(), calls=%async_computation.10 | async-start | bytes 663552 | tf_op jit(solution)/shard_map/reduce_scatter | solution.py:114
  518.3 99.7 %reduce-scatter.8.cloned.1.call-start = ((), (), s32[]{:S(2)}) async-start(), calls=%async_computation.11 | async-start | bytes 663552 | tf_op jit(solution)/shard_map/reduce_scatter | solution.py:114
Sparse Core Ops, SparseCore 0:
  88.4 124.4 all-reduce.8
  431.6 30.1 reduce-scatter.3
  518.4 28.2 reduce-scatter.5
  590.0 27.9 reduce-scatter.7
where the time goes:
time: 631 us; the launch traced here: 626 us
  waiting for transfers between devices  154 us (24%)
  local copies, waits for them, and re-layouts  127 us (20%)
  blocking collectives  118 us (19%)
  matrix products  110 us (17%)
  other arithmetic  81.1 us (13%)
  starting transfers between devices  21.8 us (3%)
  between operations  14.1 us (2%)
    unnamed x5, waiting for transfers between devices  116 us
    all_gather x3, blocking collectives, per_device(): all_rows = lax.all_gather(returned, 'gx', axis=0, tiled=True)  69.6 us
    dot_general x24, matrix products, one_block(): jnp.einsum('rhk,rkd->rhd', weights.astype(jnp.bfloat16), values, preferre...  53.9 us
    unnamed x46, local copies, waits for them, and re-layouts  52 us
    dot_general x24, matrix products, one_block(): jnp.einsum('rhd,rkd->rhk', queries, keys, preferred_element_type=jnp.floa...  42.4 us
    all_gather x3, blocking collectives, per_device(): gathered = lax.all_gather(step_tokens, 'gy', axis=0, tiled=True)  40.2 us
    scatter x12, other arithmetic  35.7 us
    reduce_scatter x3, waiting for transfers between devices, per_device(): lax.psum_scatter(jnp.einsum('rsh,hd->rsd', all_rows, out_weight, preferre...  28.1 us
  transfers between devices with their start and end apart: 9, of which 5 were waited for; matrix products, arithmetic and copies ran while one was open for 34% of the time, Pallas kernels for 0%

commit v1 on v0

v1 whole, which is shorter than its diff:
```python
import functools

import jax
import jax.numpy as jnp
from jax import lax
from jax.experimental import pallas as pl
from jax.experimental.pallas import tpu as pltpu
from jax.sharding import PartitionSpec as P

STEPS = 3
LANES = 128
HEAD = 256
SLOT_BLOCK = 1024
MESSAGE = 40
LOG2_E = 1.4426950408889634
VMEM_BYTES = 56 * 1024 * 1024


def across(step_y, step_core):
    count = lax.axis_size("gy")
    ring = count // 2
    return [
        (place, (place // 2 + step_y) % ring * 2 + (place % 2 + step_core) % 2)
        for place in range(count)
    ]


def move(value, step_y, step_core):
    return lax.ppermute(value, "gy", across(step_y, step_core))


def gather_tokens(own):
    half = own.shape[0] // 2
    above = move(own, 1, 0)
    below = move(own, -1, 0)
    other = move(own, 0, 1)
    far_front = move(above[:half], 1, 0)
    far_back = move(below[half:], -1, 0)
    other_above = move(above, 0, 1)
    other_below = move(below, 0, 1)
    far = jnp.concatenate([far_front, far_back], 0)
    other_far = move(far, 0, 1)
    ring = lax.axis_size("gy") // 2
    here = lax.axis_index("gy")
    y, core = here // 2, here % 2
    places = [
        (y + shift) % ring * 2 + (core + flip) % 2
        for shift, flip in [(0, 0), (0, 1), (-1, 0), (1, 0), (-1, 1), (1, 1), (2, 0), (2, 1)]
    ]
    blocks = [own, other, above, below, other_above, other_below, far, other_far]
    return blocks, jnp.stack(places).astype(jnp.int32)


def project_kernel(places, *refs):
    blocks = refs[:8]
    q_weight, kv_weight, out, gathered, spread = refs[8:]
    rows = blocks[0].shape[0]
    requests = rows // STEPS
    for index, block in enumerate(blocks):
        gathered[index * rows : (index + 1) * rows, :] = block[...]
    heads = q_weight.shape[1] // HEAD
    for part in range(heads + 1):
        if part < heads:
            weight = q_weight[:, part * HEAD : (part + 1) * HEAD]
        else:
            weight = kv_weight[...]
        partial = jnp.dot(gathered[...], weight, preferred_element_type=jnp.float32)
        for index in range(8):
            for step in range(STEPS):
                start = index * rows + step * requests
                piece = partial[start : start + requests]
                if part < heads:
                    spots = (step * heads + part, STEPS * heads + step * heads + part)
                else:
                    spots = (2 * STEPS * heads + step,)
                for side, spot in enumerate(spots):
                    spread[pl.ds(index * requests * MESSAGE + spot, requests, stride=MESSAGE), :] = (
                        piece[:, side * LANES : (side + 1) * LANES]
                    )
    for index in range(8):
        size = requests * MESSAGE
        first = pl.multiple_of(places[index] * size, size)
        out[pl.ds(first, size), :] = spread[index * size : (index + 1) * size, :].astype(out.dtype)


def project(places, blocks, q_weight, kv_weight):
    rows = blocks[0].shape[0]
    requests = rows // STEPS * 8
    vmem = pl.BlockSpec(memory_space=pltpu.VMEM)
    return pl.pallas_call(
        project_kernel,
        out_shape=jax.ShapeDtypeStruct((requests * MESSAGE, LANES), jnp.bfloat16),
        in_specs=[pl.BlockSpec(memory_space=pltpu.SMEM)] + [vmem] * 10,
        out_specs=vmem,
        scratch_shapes=[
            pltpu.VMEM((rows * 8, blocks[0].shape[1]), jnp.bfloat16),
            pltpu.VMEM((requests * MESSAGE, LANES), jnp.float32),
        ],
        compiler_params=pltpu.CompilerParams(vmem_limit_bytes=VMEM_BYTES),
        name="project",
    )(places, *blocks, q_weight, kv_weight)


def attend_kernel(lengths, partials, cosine, sine, cache, out, store, summed, query, replies, arrived):
    group = out.shape[1]
    peers = out.shape[0]
    requests, slots, _ = cache.shape
    blocks = slots // SLOT_BLOCK
    heads_rows = (MESSAGE - 4) // 2
    total_rows = group * heads_rows

    def fetch(request, block):
        place = pl.ds(block * SLOT_BLOCK, SLOT_BLOCK)
        return pltpu.make_async_copy(
            cache.at[request, place], store.at[request, place], arrived.at[request, block]
        )

    for block in range(blocks):
        for request in range(requests):

            @pl.when(block * SLOT_BLOCK < lengths[request])
            def _(request=request, block=block):
                fetch(request, block).start()

    for place in range(group):
        total = partials[0, place].astype(jnp.float32)
        for peer in range(1, peers):
            total = total + partials[peer, place].astype(jnp.float32)
        summed[place] = total.astype(jnp.bfloat16).astype(jnp.float32)

    replies[...] = jnp.zeros_like(replies)
    row_step = lax.broadcasted_iota(jnp.int32, (total_rows, LANES), 0) % heads_rows // (heads_rows // STEPS)
    column = lax.broadcasted_iota(jnp.int32, (total_rows, LANES), 1)
    scale = jnp.float32(LOG2_E / 16.0)
    for request in range(requests):
        base = request * MESSAGE
        cos_rows = cosine[request, :heads_rows]
        sin_rows = sine[request, :heads_rows]
        for place in range(group):
            front = summed[place, base : base + heads_rows]
            back = summed[place, base + heads_rows : base + 2 * heads_rows]
            target = pl.ds(place * heads_rows, heads_rows)
            query[target, :LANES] = front * cos_rows - back * sin_rows
            query[target, LANES:] = back * cos_rows + front * sin_rows
        queries = query[...].astype(jnp.bfloat16)

        new = pl.ds(base + 2 * heads_rows, STEPS)
        key_cos = cosine[request, heads_rows : heads_rows + STEPS]
        key_sin = sine[request, heads_rows : heads_rows + STEPS]
        front, back = summed[0, new], summed[group // 4, new]
        new_keys = jnp.concatenate(
            [front * key_cos - back * key_sin, back * key_cos + front * key_sin], -1
        )
        new_values = jnp.concatenate([summed[group // 2, new], summed[3 * group // 4, new]], -1)
        padding = jnp.zeros((LANES - STEPS, HEAD), jnp.float32)
        new_keys = jnp.concatenate([new_keys, padding], 0).astype(jnp.bfloat16)
        new_values = jnp.concatenate([new_values, padding], 0).astype(jnp.bfloat16)

        scores = lax.dot_general(
            queries, new_keys, (((1,), (1,)), ((), ())), preferred_element_type=jnp.float32
        ) * scale
        scores = jnp.where(column <= row_step, scores, jnp.float32(-1e30))
        top = jnp.max(scores, axis=-1, keepdims=True)
        weights = jnp.exp2(scores - top)
        denom = jnp.sum(weights, axis=-1, keepdims=True)
        accum = jnp.dot(weights.astype(jnp.bfloat16), new_values, preferred_element_type=jnp.float32)

        length = lengths[request]

        def one_block(block, state, request=request, queries=queries, length=length):
            top, denom, accum = state
            fetch(request, block).wait()
            place = pl.ds(pl.multiple_of(block * SLOT_BLOCK, SLOT_BLOCK), SLOT_BLOCK)
            keys = store[request, place, :HEAD]
            values = store[request, place, HEAD:]
            slot = block * SLOT_BLOCK + lax.broadcasted_iota(jnp.int32, (1, SLOT_BLOCK), 1)
            hidden = jnp.where(slot < length, jnp.float32(0.0), jnp.float32(-1e30))
            scores = lax.dot_general(
                queries, keys, (((1,), (1,)), ((), ())), preferred_element_type=jnp.float32
            ) * scale + hidden
            new_top = jnp.maximum(top, jnp.max(scores, axis=-1, keepdims=True))
            weights = jnp.exp2(scores - new_top)
            factor = jnp.exp2(top - new_top)
            denom = denom * factor + jnp.sum(weights, axis=-1, keepdims=True)
            accum = accum * factor + jnp.dot(
                weights.astype(jnp.bfloat16), values, preferred_element_type=jnp.float32
            )
            return new_top, denom, accum

        needed = (length + SLOT_BLOCK - 1) // SLOT_BLOCK
        top, denom, accum = lax.fori_loop(0, needed, one_block, (top, denom, accum))
        query[...] = accum / denom
        for place in range(group):
            source = pl.ds(place * heads_rows, heads_rows)
            replies[place, base : base + heads_rows] = query[source, :LANES]
            replies[place, base + heads_rows : base + 2 * heads_rows] = query[source, LANES:]

    for place in range(group):
        reply = replies[place].astype(jnp.bfloat16)
        for peer in range(peers):
            out[peer, place] = reply


def attend(lengths, partials, cosine, sine, cache):
    peers, group, rows, _ = partials.shape
    requests, slots, width = cache.shape
    vmem = pl.BlockSpec(memory_space=pltpu.VMEM)
    return pl.pallas_call(
        attend_kernel,
        out_shape=jax.ShapeDtypeStruct(partials.shape, jnp.bfloat16),
        in_specs=[
            pl.BlockSpec(memory_space=pltpu.SMEM),
            vmem,
            vmem,
            vmem,
            pl.BlockSpec(memory_space=pl.ANY),
        ],
        out_specs=vmem,
        scratch_shapes=[
            pltpu.VMEM((requests, slots, width), jnp.bfloat16),
            pltpu.VMEM((group, rows, LANES), jnp.float32),
            pltpu.VMEM((group * (MESSAGE - 4) // 2, HEAD), jnp.float32),
            pltpu.VMEM((group, rows, LANES), jnp.float32),
            pltpu.SemaphoreType.DMA((requests, slots // SLOT_BLOCK)),
        ],
        compiler_params=pltpu.CompilerParams(vmem_limit_bytes=VMEM_BYTES),
        name="attend",
    )(lengths, partials, cosine, sine, cache)


def output_kernel(places, attended, out_weight, out, spread, rows_ref):
    blocks, rows, width = out.shape
    requests = rows // STEPS
    heads = out_weight.shape[0] // HEAD
    size = requests * MESSAGE
    for index in range(blocks):
        first = pl.multiple_of(places[index] * size, size)
        spread[...] = attended[pl.ds(first, size), :].astype(jnp.float32)
        for step in range(STEPS):
            for head in range(heads):
                for side in range(2):
                    spot = side * STEPS * heads + step * heads + head
                    lane = head * HEAD + side * LANES
                    start = index * rows + step * requests
                    rows_ref[start : start + requests, lane : lane + LANES] = spread[
                        pl.ds(spot, requests, stride=MESSAGE), :
                    ].astype(jnp.bfloat16)
    for first in range(0, width, HEAD):
        size = min(HEAD, width - first)
        partial = jnp.dot(
            rows_ref[...], out_weight[:, first : first + size], preferred_element_type=jnp.float32
        ).astype(jnp.bfloat16)
        for index in range(blocks):
            out[index, :, first : first + size] = partial[index * rows : (index + 1) * rows]


def output_partial(places, attended, out_weight, rows):
    blocks = places.shape[0]
    vmem = pl.BlockSpec(memory_space=pltpu.VMEM)
    return pl.pallas_call(
        output_kernel,
        out_shape=jax.ShapeDtypeStruct((blocks, rows, out_weight.shape[1]), jnp.bfloat16),
        in_specs=[pl.BlockSpec(memory_space=pltpu.SMEM), vmem, vmem],
        out_specs=vmem,
        scratch_shapes=[
            pltpu.VMEM((rows // STEPS * MESSAGE, LANES), jnp.float32),
            pltpu.VMEM((blocks * rows, out_weight.shape[0]), jnp.bfloat16),
        ],
        compiler_params=pltpu.CompilerParams(vmem_limit_bytes=VMEM_BYTES),
        name="output",
    )(places, attended, out_weight)


def plus(first, second):
    return (first.astype(jnp.float32) + second.astype(jnp.float32)).astype(jnp.bfloat16)


def per_device(tokens, q_weight, kv_weight, out_weight, kv_cache, lengths):
    gx_count, gy_count = lax.axis_size("gx"), lax.axis_size("gy")
    here = lax.axis_index("gy")
    y, core = here // 2, here % 2
    ring = gy_count // 2
    steps, block_requests, depth = tokens.shape
    rows = steps * block_requests
    req_local = kv_cache.shape[0]
    heads_local = q_weight.shape[1] // HEAD
    kv_columns = kv_weight.shape[1] // ring

    own_kv = lax.dynamic_slice_in_dim(kv_weight, y * kv_columns, kv_columns, 1)
    positions = (lengths[:, None] + jnp.arange(STEPS, dtype=jnp.int32)[None, :]).astype(jnp.float32)
    half = HEAD // 2
    frequency = 10000.0 ** (-(jnp.arange(half, dtype=jnp.float32) * 2.0 / HEAD))
    angles = positions[..., None] * frequency

    def table(values):
        per_head = jnp.repeat(values, heads_local, axis=1)
        filler = jnp.zeros((req_local, 24 - STEPS - STEPS * heads_local, half), jnp.float32)
        return jnp.concatenate([per_head, values, filler], 1)

    cosine, sine = table(jnp.cos(angles)), table(jnp.sin(angles))

    blocks, places = gather_tokens(tokens.reshape(rows, depth))
    sent = project(places, blocks, q_weight, own_kv)
    everywhere = ("gx", "gy")
    sent = sent.reshape(gx_count * gy_count, req_local * MESSAGE, LANES)
    partials = lax.all_to_all(sent, everywhere, split_axis=0, concat_axis=0, tiled=True)
    partials = partials.reshape(gx_count, gy_count, req_local * MESSAGE, LANES)
    attended = attend(lengths, partials, cosine, sine, kv_cache)
    attended = attended.reshape(gx_count * gy_count, req_local * MESSAGE, LANES)
    attended = lax.all_to_all(attended, everywhere, split_axis=0, concat_axis=0, tiled=True)
    attended = attended.reshape(-1, LANES)

    shifts = jnp.arange(ring, dtype=jnp.int32)
    ahead = (y + shifts) % ring * 2
    for_other = output_partial(ahead + 1 - core, attended, out_weight, rows)
    from_other = move(for_other, 0, 1)
    mine = output_partial(ahead + core, attended, out_weight, rows)
    mine = plus(mine, from_other)
    cut = rows // 2
    front = move(mine[2, :cut], 1, 0)
    back = move(mine[2, cut:], -1, 0)
    up = jnp.concatenate([plus(mine[1, :cut], front), mine[1, cut:]], 0)
    down = jnp.concatenate([mine[3, :cut], plus(mine[3, cut:], back)], 0)
    from_below = move(up, 1, 0)
    from_above = move(down, -1, 0)
    result = (
        mine[0].astype(jnp.float32)
        + from_below.astype(jnp.float32)
        + from_above.astype(jnp.float32)
    ).astype(jnp.bfloat16)
    return result.reshape(steps, block_requests, -1)


def solution(mesh):
    in_specs = (
        P(None, "gy", "gx"),
        P("gx", "gy"),
        P("gx", None),
        P("gy", "gx"),
        P(("gx", "gy"), None, None),
        P(("gx", "gy")),
    )
    out_specs = P(None, "gy", "gx")
    return jax.shard_map(
        per_device, mesh=mesh, in_specs=in_specs, out_specs=out_specs, check_vma=False
    )
```

time: 631 us -> 161 us (0.26)
  local copies, waits for them, and re-layouts: 127 us -> 2.48 us
  blocking collectives: 118 us -> 0 us
  matrix products: 110 us -> 0 us
  other arithmetic: 81.1 us -> 4.18 us
  waiting for transfers between devices: 154 us -> 87.9 us
  Pallas kernels: 0 us -> 31.4 us
  between operations: 14.1 us -> 0.21 us
  starting transfers between devices: 21.8 us -> 34.2 us
    unnamed x5 -> x0, waiting for transfers between devices: 116 us -> none
    dot_general x54 -> x0, matrix products: 110 us -> none  [the longest x24 53.9 us: one_block(): jnp.einsum('rhk,rkd->rhd', weights.astype(jnp.bfloat16), values, preferre...]
    all_gather x6 -> x0, blocking collectives: 110 us -> none  [the longest x3 69.6 us: per_device(): all_rows = lax.all_gather(returned, 'gx', axis=0, tiled=True)]
    all_to_all x5 -> x2, waiting for transfers between devices: 9.77 us -> 69.8 us  [the longest x1 35.2 us: per_device(): lax.all_to_all(attended, everywhere, split_axis=0, concat_axis=0, tiled=T...]
    unnamed x46 -> x19, local copies, waits for them, and re-layouts: 52 us -> 0.86 us
    scatter x13 -> x0, other arithmetic: 36.3 us -> none
    pallas_call x0 -> x4, Pallas kernels: none -> 31.4 us  [the longest x2 12 us: output_partial(): pl.pallas_call(output_kernel, out_shape=jax.ShapeDtypeStruct((blocks, row...]
    reduce_scatter x3 -> x0, waiting for transfers between devices: 28.1 us -> none  [per_device(): lax.psum_scatter(jnp.einsum('rsh,hd->rsd', all_rows, out_weight, preferre...]
  transfers between devices with their start and end apart: 9 -> 15, of which waited for: 5 -> 9; matrix products, arithmetic and copies ran while one was open for 34% -> 2% of each run, Pallas kernels for 0% -> 4%
where the time goes in v1:
time: 161 us; the launch traced here: 160 us
  waiting for transfers between devices  87.9 us (55%)
  starting transfers between devices  34.2 us (21%)
  Pallas kernels  31.4 us (20%)
  other arithmetic  4.18 us (3%)
  local copies, waits for them, and re-layouts  2.48 us (2%)
    all_to_all x1, waiting for transfers between devices, per_device(): lax.all_to_all(attended, everywhere, split_axis=0, concat_axis=0, tiled=T...  35.2 us
    all_to_all x1, waiting for transfers between devices, per_device(): lax.all_to_all(sent, everywhere, split_axis=0, concat_axis=0, tiled=True)  34.6 us
    ppermute x13, waiting for transfers between devices, move(): return lax.ppermute(value, 'gy', across(step_y, step_core))  18.1 us
    ppermute x13, starting transfers between devices, move(): return lax.ppermute(value, 'gy', across(step_y, step_core))  12.7 us
    all_to_all x1, starting transfers between devices, per_device(): lax.all_to_all(sent, everywhere, split_axis=0, concat_axis=0, tiled=True)  12.1 us
    pallas_call x2, Pallas kernels, output_partial(): pl.pallas_call(output_kernel, out_shape=jax.ShapeDtypeStruct((blocks, row...  12 us
    pallas_call x1, Pallas kernels, attend(): pl.pallas_call(attend_kernel, out_shape=jax.ShapeDtypeStruct(partials.sha...  11.3 us
    all_to_all x1, starting transfers between devices, per_device(): lax.all_to_all(attended, everywhere, split_axis=0, concat_axis=0, tiled=T...  9.44 us
  transfers between devices with their start and end apart: 15, of which 9 were waited for; matrix products, arithmetic and copies ran while one was open for 2% of the time, Pallas kernels for 4%

profile of v1, /device:TPU:0, one launch (start us, length us, event | category | flops | bytes accessed | tf_op | source)
XLA Modules:
  0.0 160.5 jit_solution(15554065631250180031)
XLA Ops:
  0.0 1.7 %collective-permute-start.1 = (bf16[96,1152]{1,0:T(8,128)(2,1)}, bf16[96,1152]{1,0:T(8,128)(2,1)S(1)}, u32[]{:S(2)}, u32[]{:S(2)}) collective-permute-start(bf16[96,1152]{1,0:T(8,128)(2,1)} %bitcast.41), channel_id=1, source_target_pairs={{0,2},{1,3},{2,4},{3,5},{4,6},{5,7},{6,0},{7,1},{8,10},{9,11},{10,... | collective-permute-start | bytes 663560 | tf_op jit(solution)/shard_map/ppermute | solution.py:29
  1.7 1.6 collective-permute-start.2
  3.2 5.5 %collective-permute-done.1.refs_2_ = bf16[96,1152]{1,0:T(8,128)(2,1)S(1)} collective-permute-done((bf16[96,1152]{1,0:T(8,128)(2,1)}, bf16[96,1152]{1,0:T(8,128)(2,1)S(1)}, u32[]{:S(2)}, u32[]{:S(2)}) %collective-permute-start.1) | collective-permute-done | bytes 221216 | tf_op jit(solution)/shard_map/ppermute | solution.py:29
  8.8 0.4 collective-permute-start.5
  9.1 0.0 collective-permute-start
  9.1 0.7 stack.35.places
  9.8 0.0 collective-permute-done.2.refs_3_
  9.8 3.0 %collective-permute-start.6 = (bf16[48,1152]{1,0:T(8,128)(2,1)S(1)}, bf16[48,1152]{1,0:T(8,128)(2,1)S(1)}, u32[]{:S(2)}, u32[]{:S(2)}) collective-permute-start(bf16[48,1152]{1,0:T(8,128)(2,1)S(1)} %slice.37), channel_id=1, source_target_pairs={{0,6},{1,7},{2,0},{3,1},{4,2},{5,3},{6,4},{7,5},{8,14},{9,15},{10,... | collective-permute-start | bytes 331784 | tf_op jit(solution)/shard_map/ppermute | solution.py:29
  12.8 0.2 collective-permute-start.3
  13.0 0.3 collective-permute-start.4
  13.3 1.5 collective-permute-done.5
  14.8 1.0 collective-permute-done.6
  15.8 0.1 collective-permute-start.7
  15.9 0.8 constant_dynamic-slice_fusion.refs_9_
  16.7 0.0 collective-permute-done.refs_1_
  16.7 0.0 collective-permute-done.4.refs_5_
  16.7 0.6 collective-permute-done.7.refs_7_
  17.4 0.0 copy-done.4
  17.4 0.1 copy-done.5
  17.5 0.1 copy-done.6
  17.5 0.7 copy-done.7
  18.2 8.2 %project.1 = bf16[10240,128]{1,0:T(8,128)(2,1)} custom-call(s32[8]{0:T(128)} %stack.35.places, bf16[96,1152]{1,0:T(8,128)(2,1)} %bitcast.44, bf16[96,1152]{1,0:T(8,128)(2,1)} %copy-done.4, bf16[96,1152]{1,0:T(8,128)(2,1)} %copy-done.1, bf16[96,1152]{1,0:T(8,128)(2,1)} %copy-done.2, bf16[96,1152]{1,0:T(8,128)(2,1)} %copy-done.5, bf16[96,1152]{1,0:T(8,128)(2,1)} %copy-done.6, ...), custom_call_target="tpu_custom_call" | custom-call | tf_op jit(solution)/shard_map/project/pallas_call | solution.py:90
  26.4 12.1 %all-to-all-start = ((bf16[128,80,128]{2,1,0:T(8,128)(2,1)}), bf16[128,80,128]{2,1,0:T(8,128)(2,1)}, u32[]{:S(2)}, u32[]{:S(2)}) async-start(bf16[128,80,128]{2,1,0:T(8,128)(2,1)} %bitcast.39), calls=%async_computation | async-start | bytes 5242880 | tf_op jit(solution)/shard_map/all_to_all | solution.py:306
  38.6 0.1 add_convert_fusion.1
  38.6 0.1 multiply_sine_fusion
  38.8 0.1 pad.9.clone
  38.9 0.7 maximum_maximum_fusion.1
  39.6 34.6 %all-to-all-done = bf16[128,80,128]{2,1,0:T(8,128)(2,1)} async-done(((bf16[128,80,128]{2,1,0:T(8,128)(2,1)}), bf16[128,80,128]{2,1,0:T(8,128)(2,1)}, u32[]{:S(2)}, u32[]{:S(2)}) %all-to-all-start) | async-done | bytes 2621472 | tf_op jit(solution)/shard_map/all_to_all | solution.py:306
  74.2 11.3 %attend.1 = bf16[16,8,80,128]{3,2,1,0:T(8,128)(2,1)} custom-call(s32[2]{0:T(128)} %lengths.1, bf16[16,8,80,128]{3,2,1,0:T(8,128)(2,1)} %bitcast.10.partials, f32[2,24,128]{2,1,0:T(8,128)} %get-tuple-element.14.cosine, f32[2,24,128]{2,1,0:T(8,128)} %get-tuple-element.13.sine, bf16[2,8192,512]{2,1,0:T(8,128)(2,1)} %cache.1), custom_call_target="tpu_custom_call" | custom-call | tf_op jit(solution)/shard_map/attend/pallas_call | solution.py:208
  85.5 9.4 %all-to-all-start.1 = ((bf16[128,80,128]{2,1,0:T(8,128)(2,1)}), bf16[128,80,128]{2,1,0:T(8,128)(2,1)}, u32[]{:S(2)}, u32[]{:S(2)}) async-start(bf16[128,80,128]{2,1,0:T(8,128)(2,1)} %bitcast.40), calls=%async_computation.1 | async-start | bytes 5242880 | tf_op jit(solution)/shard_map/all_to_all | solution.py:310
  95.0 0.5 add_subtract_fusion.places
  95.5 35.2 %all-to-all-done.1 = bf16[128,80,128]{2,1,0:T(8,128)(2,1)} async-done(((bf16[128,80,128]{2,1,0:T(8,128)(2,1)}), bf16[128,80,128]{2,1,0:T(8,128)(2,1)}, u32[]{:S(2)}, u32[]{:S(2)}) %all-to-all-start.1) | async-done | bytes 2621472 | tf_op jit(solution)/shard_map/all_to_all | solution.py:310
  130.7 6.0 %output.3 = bf16[4,96,1152]{2,1,0:T(8,128)(2,1)} custom-call(s32[4]{0:T(128)} %add_subtract_fusion.places, bf16[10240,128]{1,0:T(8,128)(2,1)} %bitcast.14.attended, bf16[1536,1152]{1,0:T(8,128)(2,1)} %out_weight.3), custom_call_target="tpu_custom_call" | custom-call | tf_op jit(solution)/shard_map/output/pallas_call | solution.py:260
  136.7 0.0 collective-permute-start.8
  136.7 0.5 broadcast_add_fusion.places
  137.2 6.0 %output.2 = bf16[4,96,1152]{2,1,0:T(8,128)(2,1)} custom-call(s32[4]{0:T(128)} %broadcast_add_fusion.places, bf16[10240,128]{1,0:T(8,128)(2,1)} %bitcast.14.attended, bf16[1536,1152]{1,0:T(8,128)(2,1)} %out_weight.3), custom_call_target="tpu_custom_call" | custom-call | tf_op jit(solution)/shard_map/output/pallas_call | solution.py:260
  143.2 0.0 collective-permute-done.8
  143.2 1.4 add_convert_fusion
  144.6 0.6 collective-permute-start.11
  145.2 1.5 collective-permute-start.9
  146.7 3.4 %collective-permute-done.11 = bf16[48,1152]{1,0:T(8,128)(2,1)S(1)} collective-permute-done((bf16[48,1152]{1,0:T(8,128)(2,1)S(1)}, bf16[48,1152]{1,0:T(8,128)(2,1)S(1)}, u32[]{:S(2)}, u32[]{:S(2)}) %collective-permute-start.11) | collective-permute-done | bytes 110624 | tf_op jit(solution)/shard_map/ppermute | solution.py:29
  150.2 1.4 collective-permute-done.9
  151.6 0.1 fusion.3
  151.7 0.4 collective-permute-start.10
  152.1 3.0 %collective-permute-start.12 = (bf16[96,1152]{1,0:T(8,128)(2,1)S(1)}, bf16[96,1152]{1,0:T(8,128)(2,1)S(1)}, u32[]{:S(2)}, u32[]{:S(2)}) collective-permute-start(bf16[96,1152]{1,0:T(8,128)(2,1)S(1)} %pad_maximum_fusion.1), channel_id=1, source_target_pairs={{0,6},{1,7},{2,0},{3,1},{4,2},{5,3},{6,4},{7,5},{8,14},{9,15},{10,... | collective-permute-start | bytes 663560 | tf_op jit(solution)/shard_map/ppermute | solution.py:29
  155.1 4.6 %collective-permute-done.10 = bf16[96,1152]{1,0:T(8,128)(2,1)S(1)} collective-permute-done((bf16[96,1152]{1,0:T(8,128)(2,1)S(1)}, bf16[96,1152]{1,0:T(8,128)(2,1)S(1)}, u32[]{:S(2)}, u32[]{:S(2)}) %collective-permute-start.10) | collective-permute-done | bytes 221216 | tf_op jit(solution)/shard_map/ppermute | solution.py:29
  159.7 0.0 collective-permute-done.12
  159.7 0.8 fusion.1
  (30 shorter events, 0.2 us)
Async XLA Ops:
  0.0 15.9 %copy-start = (bf16[1152,512]{1,0:T(8,128)(2,1)S(1)}, bf16[1152,512]{1,0:T(8,128)(2,1)}, u32[]{:S(2)}) copy-start(bf16[1152,512]{1,0:T(8,128)(2,1)} %param.8) | copy-start | bytes 3538948
  0.0 8.7 %collective-permute-start.1 = (bf16[96,1152]{1,0:T(8,128)(2,1)}, bf16[96,1152]{1,0:T(8,128)(2,1)S(1)}, u32[]{:S(2)}, u32[]{:S(2)}) collective-permute-start(bf16[96,1152]{1,0:T(8,128)(2,1)} %bitcast.41), channel_id=1, source_target_pairs={{0,2},{1,3},{2,4},{3,5},{4,6},{5,7},{6,0},{7,1},{8,10},{9,11},{10,... | collective-permute-start | bytes 663560 | tf_op jit(solution)/shard_map/ppermute | solution.py:29
  1.7 8.1 %collective-permute-start.2 = (bf16[96,1152]{1,0:T(8,128)(2,1)}, bf16[96,1152]{1,0:T(8,128)(2,1)S(1)}, u32[]{:S(2)}, u32[]{:S(2)}) collective-permute-start(bf16[96,1152]{1,0:T(8,128)(2,1)} %bitcast.42), channel_id=1, source_target_pairs={{0,6},{1,7},{2,0},{3,1},{4,2},{5,3},{6,4},{7,5},{8,14},{9,15},{10,... | collective-permute-start | bytes 663560 | tf_op jit(solution)/shard_map/ppermute | solution.py:29
  8.7 8.6 %copy-start.1 = (bf16[96,1152]{1,0:T(8,128)(2,1)}, bf16[96,1152]{1,0:T(8,128)(2,1)S(1)}, u32[]{:S(2)}) copy-start(bf16[96,1152]{1,0:T(8,128)(2,1)S(1)} %collective-permute-done.1.refs_2_) | copy-start | bytes 663556
  8.8 6.0 %collective-permute-start.5 = (bf16[48,1152]{1,0:T(8,128)(2,1)S(1)}, bf16[48,1152]{1,0:T(8,128)(2,1)S(1)}, u32[]{:S(2)}, u32[]{:S(2)}) collective-permute-start(bf16[48,1152]{1,0:T(8,128)(2,1)S(1)} %slice.36), channel_id=1, source_target_pairs={{0,2},{1,3},{2,4},{3,5},{4,6},{5,7},{6,0},{7,1},{8,10},{9,11},{10,... | collective-permute-start | bytes 331784 | tf_op jit(solution)/shard_map/ppermute | solution.py:29
  9.1 7.6 %collective-permute-start = (bf16[96,1152]{1,0:T(8,128)(2,1)}, bf16[96,1152]{1,0:T(8,128)(2,1)S(1)}, u32[]{:S(2)}, u32[]{:S(2)}) collective-permute-start(bf16[96,1152]{1,0:T(8,128)(2,1)} %bitcast.43), channel_id=1, source_target_pairs={{0,1},{1,0},{2,3},{3,2},{4,5},{5,4},{6,7},{7,6},{8,9},{9,8},{10,11... | collective-permute-start | bytes 663560 | tf_op jit(solution)/shard_map/ppermute | solution.py:29
  9.8 7.6 %copy-start.2 = (bf16[96,1152]{1,0:T(8,128)(2,1)}, bf16[96,1152]{1,0:T(8,128)(2,1)S(1)}, u32[]{:S(2)}) copy-start(bf16[96,1152]{1,0:T(8,128)(2,1)S(1)} %collective-permute-done.2.refs_3_) | copy-start | bytes 663556
  9.8 6.0 %collective-permute-start.6 = (bf16[48,1152]{1,0:T(8,128)(2,1)S(1)}, bf16[48,1152]{1,0:T(8,128)(2,1)S(1)}, u32[]{:S(2)}, u32[]{:S(2)}) collective-permute-start(bf16[48,1152]{1,0:T(8,128)(2,1)S(1)} %slice.37), channel_id=1, source_target_pairs={{0,6},{1,7},{2,0},{3,1},{4,2},{5,3},{6,4},{7,5},{8,14},{9,15},{10,... | collective-permute-start | bytes 331784 | tf_op jit(solution)/shard_map/ppermute | solution.py:29
  12.8 3.9 %collective-permute-start.3 = (bf16[96,1152]{1,0:T(8,128)(2,1)S(1)}, bf16[96,1152]{1,0:T(8,128)(2,1)S(1)}, u32[]{:S(2)}, u32[]{:S(2)}) collective-permute-start(bf16[96,1152]{1,0:T(8,128)(2,1)S(1)} %collective-permute-done.1.refs_2_), channel_id=1, source_target_pairs={{0,1},{1,0},{2,3},{3,2},{4,5},{5,4},{6,7},{7,6},{8,9},{9,8},{10,11... | collective-permute-start | bytes 663560 | tf_op jit(solution)/shard_map/ppermute | solution.py:29
  13.0 3.7 %collective-permute-start.4 = (bf16[96,1152]{1,0:T(8,128)(2,1)S(1)}, bf16[96,1152]{1,0:T(8,128)(2,1)S(1)}, u32[]{:S(2)}, u32[]{:S(2)}) collective-permute-start(bf16[96,1152]{1,0:T(8,128)(2,1)S(1)} %collective-permute-done.2.refs_3_), channel_id=1, source_target_pairs={{0,1},{1,0},{2,3},{3,2},{4,5},{5,4},{6,7},{7,6},{8,9},{9,8},{10,11... | collective-permute-start | bytes 663560 | tf_op jit(solution)/shard_map/ppermute | solution.py:29
  15.8 1.6 copy-start.3
  15.8 1.6 collective-permute-start.7
  16.7 0.7 copy-start.4
  16.7 0.8 copy-start.5
  16.7 0.8 copy-start.6
  17.5 0.7 copy-start.7
  26.4 12.1 %copy-start.8 = (s32[2]{0:T(128)S(1)}, s32[2]{0:T(128)}, u32[]{:S(2)}) copy-start(s32[2]{0:T(128)} %lengths.1) | copy-start | bytes 28
  26.4 47.8 %all-to-all-start = ((bf16[128,80,128]{2,1,0:T(8,128)(2,1)}), bf16[128,80,128]{2,1,0:T(8,128)(2,1)}, u32[]{:S(2)}, u32[]{:S(2)}) async-start(bf16[128,80,128]{2,1,0:T(8,128)(2,1)} %bitcast.39), calls=%async_computation | async-start | bytes 5242880 | tf_op jit(solution)/shard_map/all_to_all | solution.py:306
  85.5 45.2 %all-to-all-start.1 = ((bf16[128,80,128]{2,1,0:T(8,128)(2,1)}), bf16[128,80,128]{2,1,0:T(8,128)(2,1)}, u32[]{:S(2)}, u32[]{:S(2)}) async-start(bf16[128,80,128]{2,1,0:T(8,128)(2,1)} %bitcast.40), calls=%async_computation.1 | async-start | bytes 5242880 | tf_op jit(solution)/shard_map/all_to_all | solution.py:310
  136.7 6.5 %collective-permute-start.8 = (bf16[4,96,1152]{2,1,0:T(8,128)(2,1)}, bf16[4,96,1152]{2,1,0:T(8,128)(2,1)S(1)}, u32[]{:S(2)}, u32[]{:S(2)}) collective-permute-start(bf16[4,96,1152]{2,1,0:T(8,128)(2,1)} %output.3), channel_id=1, source_target_pairs={{0,1},{1,0},{2,3},{3,2},{4,5},{5,4},{6,7},{7,6},{8,9},{9,8},{10,11... | collective-permute-start | bytes 2654216 | tf_op jit(solution)/shard_map/ppermute | solution.py:29
  144.6 5.5 %collective-permute-start.11 = (bf16[48,1152]{1,0:T(8,128)(2,1)S(1)}, bf16[48,1152]{1,0:T(8,128)(2,1)S(1)}, u32[]{:S(2)}, u32[]{:S(2)}) collective-permute-start(bf16[48,1152]{1,0:T(8,128)(2,1)S(1)} %get-tuple-element.8), channel_id=1, source_target_pairs={{0,6},{1,7},{2,0},{3,1},{4,2},{5,3},{6,4},{7,5},{8,14},{9,15},{10,... | collective-permute-start | bytes 331784 | tf_op jit(solution)/shard_map/ppermute | solution.py:29
  145.2 6.4 %collective-permute-start.9 = (bf16[48,1152]{1,0:T(8,128)(2,1)S(1)}, bf16[48,1152]{1,0:T(8,128)(2,1)S(1)}, u32[]{:S(2)}, u32[]{:S(2)}) collective-permute-start(bf16[48,1152]{1,0:T(8,128)(2,1)S(1)} %get-tuple-element.7), channel_id=1, source_target_pairs={{0,2},{1,3},{2,4},{3,5},{4,6},{5,7},{6,0},{7,1},{8,10},{9,11},{10,... | collective-permute-start | bytes 331784 | tf_op jit(solution)/shard_map/ppermute | solution.py:29
  151.7 8.0 %collective-permute-start.10 = (bf16[96,1152]{1,0:T(8,128)(2,1)S(1)}, bf16[96,1152]{1,0:T(8,128)(2,1)S(1)}, u32[]{:S(2)}, u32[]{:S(2)}) collective-permute-start(bf16[96,1152]{1,0:T(8,128)(2,1)S(1)} %pad_maximum_fusion), channel_id=1, source_target_pairs={{0,2},{1,3},{2,4},{3,5},{4,6},{5,7},{6,0},{7,1},{8,10},{9,11},{10,... | collective-permute-start | bytes 663560 | tf_op jit(solution)/shard_map/ppermute | solution.py:29
  152.1 7.6 %collective-permute-start.12 = (bf16[96,1152]{1,0:T(8,128)(2,1)S(1)}, bf16[96,1152]{1,0:T(8,128)(2,1)S(1)}, u32[]{:S(2)}, u32[]{:S(2)}) collective-permute-start(bf16[96,1152]{1,0:T(8,128)(2,1)S(1)} %pad_maximum_fusion.1), channel_id=1, source_target_pairs={{0,6},{1,7},{2,0},{3,1},{4,2},{5,3},{6,4},{7,5},{8,14},{9,15},{10,... | collective-permute-start | bytes 663560 | tf_op jit(solution)/shard_map/ppermute | solution.py:29

commit v2 on v1

v2 whole, which is shorter than its diff:
```python
import functools

import jax
import jax.numpy as jnp
from jax import lax
from jax.experimental import pallas as pl
from jax.experimental.pallas import tpu as pltpu
from jax.sharding import PartitionSpec as P

STEPS = 3
LANES = 128
HEAD = 256
SLOT_BLOCK = 4096
MESSAGE = 40
REPLY = 36
LOG2_E = 1.4426950408889634
PROJECT_VMEM = 56 * 1024 * 1024
ATTEND_VMEM = 60 * 1024 * 1024
OUTPUT_VMEM = 24 * 1024 * 1024


def across(step_y, step_core):
    count = lax.axis_size("gy")
    ring = count // 2
    return [
        (place, (place // 2 + step_y) % ring * 2 + (place % 2 + step_core) % 2)
        for place in range(count)
    ]


def move(value, step_y, step_core):
    return lax.ppermute(value, "gy", across(step_y, step_core))


def gather_and_project(own, q_weight, kv_weight, peers):
    half = own.shape[0] // 2
    ring = lax.axis_size("gy") // 2
    here = lax.axis_index("gy")
    y, core = here // 2, here % 2

    def places(*steps):
        return jnp.stack(
            [(y + shift) % ring * 2 + (core + flip) % 2 for shift, flip in steps]
        ).astype(jnp.int32)

    above = move(own, 1, 0)
    below = move(own, -1, 0)
    other = move(own, 0, 1)
    far_front = move(above[:half], 1, 0)
    far_back = move(below[half:], -1, 0)
    other_above = move(above, 0, 1)
    other_below = move(below, 0, 1)
    first = places((0, 0), (0, 1), (-1, 0), (1, 0))
    sent = project(first, [own, other, above, below], q_weight, kv_weight, peers)
    far = jnp.concatenate([far_front, far_back], 0)
    far, sent = lax.optimization_barrier((far, sent))
    other_far = move(far, 0, 1)
    second = places((-1, 1), (1, 1), (2, 0), (2, 1))
    blocks = [other_above, other_below, far, other_far]
    return project(second, blocks, q_weight, kv_weight, peers, sent)


def project_kernel(count, places, *refs):
    blocks = refs[:count]
    q_weight, kv_weight = refs[count : count + 2]
    out, gathered, spread, narrow, sent = refs[-5:]
    rows = blocks[0].shape[0]
    requests = rows // STEPS
    heads = q_weight.shape[1] // HEAD
    for index, block in enumerate(blocks):
        gathered[index * rows : (index + 1) * rows, :] = block[...]
    for part in range(heads + 1):
        if part < heads:
            weight = q_weight[:, part * HEAD : (part + 1) * HEAD]
        else:
            weight = kv_weight[...]
        partial = jnp.dot(gathered[...], weight, preferred_element_type=jnp.float32)
        for index in range(count):
            for step in range(STEPS):
                start = index * rows + step * requests
                piece = partial[start : start + requests]
                if part < heads:
                    spots = (step * heads + part, STEPS * heads + step * heads + part)
                else:
                    spots = (2 * STEPS * heads + step,)
                for side, spot in enumerate(spots):
                    spread[pl.ds(index * requests * MESSAGE + spot, requests, stride=MESSAGE), :] = (
                        piece[:, side * LANES : (side + 1) * LANES]
                    )
    size = requests * MESSAGE
    copies = []
    for index in range(count):
        here = pl.ds(index * size, size)
        narrow[here, :] = spread[here, :].astype(narrow.dtype)
        first = pl.multiple_of(places[index] * size, size)
        copies.append(
            pltpu.make_async_copy(narrow.at[here], out.at[pl.ds(first, size)], sent.at[index])
        )
        copies[-1].start()
    for copy in copies:
        copy.wait()


def project(places, blocks, q_weight, kv_weight, peers, written=None):
    count = len(blocks)
    rows, depth = blocks[0].shape
    requests = rows // STEPS
    held = requests * count * MESSAGE
    vmem = pl.BlockSpec(memory_space=pltpu.VMEM)
    in_specs = [pl.BlockSpec(memory_space=pltpu.SMEM)] + [vmem] * (count + 2)
    operands = [places, *blocks, q_weight, kv_weight]
    if written is not None:
        in_specs.append(pl.BlockSpec(memory_space=pltpu.HBM))
        operands.append(written)
    return pl.pallas_call(
        functools.partial(project_kernel, count),
        out_shape=jax.ShapeDtypeStruct((requests * peers * MESSAGE, LANES), jnp.bfloat16),
        in_specs=in_specs,
        out_specs=pl.BlockSpec(memory_space=pltpu.HBM),
        input_output_aliases={} if written is None else {len(operands) - 1: 0},
        scratch_shapes=[
            pltpu.VMEM((rows * count, depth), jnp.bfloat16),
            pltpu.VMEM((held, LANES), jnp.float32),
            pltpu.VMEM((held, LANES), jnp.bfloat16),
            pltpu.SemaphoreType.DMA((count,)),
        ],
        compiler_params=pltpu.CompilerParams(vmem_limit_bytes=PROJECT_VMEM),
        name="project",
    )(*operands)


def attend_kernel(
    lengths, partials, cosine, sine, cache, out, keys, values, summed, query, replies, narrow, score,
    arrived, sent
):
    peers, group, _, _ = partials.shape
    requests, slots, _ = cache.shape
    blocks = slots // SLOT_BLOCK
    heads_rows = REPLY // 2
    rows = group * heads_rows
    scale = jnp.float32(LOG2_E / 16.0)

    def fetch(request, side, block):
        place = pl.ds(pl.multiple_of(block * SLOT_BLOCK, SLOT_BLOCK), SLOT_BLOCK)
        return pltpu.make_async_copy(
            cache.at[request, place, pl.ds(side * HEAD, HEAD)],
            (keys, values)[side].at[request, place],
            arrived.at[request, side, block],
        )

    def start(request, side):
        if request < requests:
            for block in range(blocks):
                fetch(request, side, block).start()

    start(0, 0)
    for place in range(group):
        total = partials[0, place].astype(jnp.float32)
        for peer in range(1, peers):
            total = total + partials[peer, place].astype(jnp.float32)
        summed[place] = total.astype(jnp.bfloat16).astype(jnp.float32)

    start(1, 0)
    start(0, 1)
    row_step = lax.broadcasted_iota(jnp.int32, (rows, LANES), 0) % heads_rows // (heads_rows // STEPS)
    column = lax.broadcasted_iota(jnp.int32, (rows, LANES), 1)

    def prepare(request):
        base = request * MESSAGE
        cos_rows = cosine[request, :heads_rows]
        sin_rows = sine[request, :heads_rows]
        for place in range(group):
            front = summed[place, base : base + heads_rows]
            back = summed[place, base + heads_rows : base + 2 * heads_rows]
            target = pl.ds(place * heads_rows, heads_rows)
            query[request, target, :LANES] = front * cos_rows - back * sin_rows
            query[request, target, LANES:] = back * cos_rows + front * sin_rows
        queries = query[request].astype(jnp.bfloat16)
        new = pl.ds(base + 2 * heads_rows, STEPS)
        key_cos = cosine[request, heads_rows : heads_rows + STEPS]
        key_sin = sine[request, heads_rows : heads_rows + STEPS]
        front, back = summed[0, new], summed[group // 4, new]
        new_keys = jnp.concatenate(
            [front * key_cos - back * key_sin, back * key_cos + front * key_sin], -1
        )
        new_values = jnp.concatenate([summed[group // 2, new], summed[3 * group // 4, new]], -1)
        padding = jnp.zeros((LANES - STEPS, HEAD), jnp.float32)
        new_keys = jnp.concatenate([new_keys, padding], 0).astype(jnp.bfloat16)
        new_values = jnp.concatenate([new_values, padding], 0).astype(jnp.bfloat16)
        scores = lax.dot_general(
            queries, new_keys, (((1,), (1,)), ((), ())), preferred_element_type=jnp.float32
        )
        return queries, jnp.where(column <= row_step, scores, jnp.float32(-1e30)), new_values

    def score_block(request, queries, block, top):
        place = pl.ds(pl.multiple_of(block * SLOT_BLOCK, SLOT_BLOCK), SLOT_BLOCK)
        fetch(request, 0, block).wait()
        slot = block * SLOT_BLOCK + lax.broadcasted_iota(jnp.int32, (1, SLOT_BLOCK), 1)
        hidden = jnp.where(slot < lengths[request], jnp.float32(0.0), jnp.float32(-1e30))
        scores = hidden + lax.dot_general(
            queries, keys[request, place], (((1,), (1,)), ((), ())), preferred_element_type=jnp.float32
        )
        score[request, block] = scores
        for lane in range(0, SLOT_BLOCK, LANES):
            top = jnp.maximum(top, scores[:, lane : lane + LANES])
        return top

    def begin(new_scores, new_values, top):
        top = jnp.max(top, axis=-1, keepdims=True) * scale
        weights = jnp.exp2(new_scores * scale - top)
        mixed = jnp.dot(weights.astype(jnp.bfloat16), new_values, preferred_element_type=jnp.float32)
        return top, weights, mixed

    def mix_block(request, top, block, denom, accum):
        place = pl.ds(pl.multiple_of(block * SLOT_BLOCK, SLOT_BLOCK), SLOT_BLOCK)
        fetch(request, 1, block).wait()
        weights = jnp.exp2(score[request, block] * scale - top)
        for lane in range(0, SLOT_BLOCK, LANES):
            denom = denom + weights[:, lane : lane + LANES]
        accum = accum + jnp.dot(
            weights.astype(jnp.bfloat16), values[request, place], preferred_element_type=jnp.float32
        )
        return denom, accum

    def finish(request, denom, accum):
        query[request] = accum / jnp.sum(denom, axis=-1, keepdims=True)
        for place in range(group):
            base = (place * requests + request) * REPLY
            source = pl.ds(place * heads_rows, heads_rows)
            replies[base : base + heads_rows] = query[request, source, :LANES]
            replies[base + heads_rows : base + 2 * heads_rows] = query[request, source, LANES:]

    ready = [prepare(request) for request in range(requests)]
    queries, new_scores, _ = ready[0]
    top = lax.fori_loop(
        0, blocks, functools.partial(score_block, 0, queries), new_scores
    )
    for request in range(requests):
        _, new_scores, new_values = ready[request]
        top, denom, accum = begin(new_scores, new_values, top)
        start(request + 1, 1)
        start(request + 2, 0)
        if request + 1 < requests:
            following, following_scores, _ = ready[request + 1]

            def both(block, state, request=request, top=top, following=following):
                next_top, denom, accum = state
                next_top = score_block(request + 1, following, block, next_top)
                denom, accum = mix_block(request, top, block, denom, accum)
                return next_top, denom, accum

            top, denom, accum = lax.fori_loop(
                0, blocks, both, (following_scores, denom, accum)
            )
        else:

            def last(block, state, request=request, top=top):
                return mix_block(request, top, block, *state)

            denom, accum = lax.fori_loop(0, blocks, last, (denom, accum))
        finish(request, denom, accum)

    narrow[...] = replies[...].astype(jnp.bfloat16)
    copies = [pltpu.make_async_copy(narrow, out.at[peer], sent.at[peer]) for peer in range(peers)]
    for copy in copies:
        copy.start()
    for copy in copies:
        copy.wait()


def attend(lengths, partials, cosine, sine, cache):
    peers, group, rows, _ = partials.shape
    requests, slots, _ = cache.shape
    blocks = slots // SLOT_BLOCK
    query_rows = group * REPLY // 2
    reply_rows = group * requests * REPLY
    vmem = pl.BlockSpec(memory_space=pltpu.VMEM)
    hbm = pl.BlockSpec(memory_space=pltpu.HBM)
    return pl.pallas_call(
        attend_kernel,
        out_shape=jax.ShapeDtypeStruct((peers, reply_rows, LANES), jnp.bfloat16),
        in_specs=[pl.BlockSpec(memory_space=pltpu.SMEM), vmem, vmem, vmem, hbm],
        out_specs=hbm,
        scratch_shapes=[
            pltpu.VMEM((requests, slots, HEAD), jnp.bfloat16),
            pltpu.VMEM((requests, slots, HEAD), jnp.bfloat16),
            pltpu.VMEM((group, rows, LANES), jnp.float32),
            pltpu.VMEM((requests, query_rows, HEAD), jnp.float32),
            pltpu.VMEM((reply_rows, LANES), jnp.float32),
            pltpu.VMEM((reply_rows, LANES), jnp.bfloat16),
            pltpu.VMEM((requests, blocks, query_rows, SLOT_BLOCK), jnp.float32),
            pltpu.SemaphoreType.DMA((requests, 2, blocks)),
            pltpu.SemaphoreType.DMA((peers,)),
        ],
        compiler_params=pltpu.CompilerParams(vmem_limit_bytes=ATTEND_VMEM),
        name="attend",
    )(lengths, partials, cosine, sine, cache)


def output_kernel(places, attended, out_weight, out, spread, rows_ref):
    blocks, rows, width = out.shape
    requests = rows // STEPS
    heads = out_weight.shape[0] // HEAD
    size = requests * REPLY
    for index in range(blocks):
        first = pl.multiple_of(places[index] * size, size)
        spread[...] = attended[pl.ds(first, size), :].astype(jnp.float32)
        for step in range(STEPS):
            for head in range(heads):
                for side in range(2):
                    spot = side * STEPS * heads + step * heads + head
                    lane = head * HEAD + side * LANES
                    start = index * rows + step * requests
                    rows_ref[start : start + requests, lane : lane + LANES] = spread[
                        pl.ds(spot, requests, stride=REPLY), :
                    ].astype(jnp.bfloat16)
    for first in range(0, width, HEAD):
        size = min(HEAD, width - first)
        partial = jnp.dot(
            rows_ref[...], out_weight[:, first : first + size], preferred_element_type=jnp.float32
        ).astype(jnp.bfloat16)
        for index in range(blocks):
            out[index, :, first : first + size] = partial[index * rows : (index + 1) * rows]


def output_partial(places, attended, out_weight, rows):
    blocks = places.shape[0]
    vmem = pl.BlockSpec(memory_space=pltpu.VMEM)
    return pl.pallas_call(
        output_kernel,
        out_shape=jax.ShapeDtypeStruct((blocks, rows, out_weight.shape[1]), jnp.bfloat16),
        in_specs=[pl.BlockSpec(memory_space=pltpu.SMEM), vmem, vmem],
        out_specs=vmem,
        scratch_shapes=[
            pltpu.VMEM((rows // STEPS * REPLY, LANES), jnp.float32),
            pltpu.VMEM((blocks * rows, out_weight.shape[0]), jnp.bfloat16),
        ],
        compiler_params=pltpu.CompilerParams(vmem_limit_bytes=OUTPUT_VMEM),
        name="output",
    )(places, attended, out_weight)


def plus(first, second):
    return (first.astype(jnp.float32) + second.astype(jnp.float32)).astype(jnp.bfloat16)


def per_device(tokens, q_weight, kv_weight, out_weight, kv_cache, lengths):
    gx_count, gy_count = lax.axis_size("gx"), lax.axis_size("gy")
    here = lax.axis_index("gy")
    y, core = here // 2, here % 2
    ring = gy_count // 2
    steps, block_requests, depth = tokens.shape
    rows = steps * block_requests
    req_local = kv_cache.shape[0]
    heads_local = q_weight.shape[1] // HEAD
    kv_columns = kv_weight.shape[1] // ring

    own_kv = lax.dynamic_slice_in_dim(kv_weight, y * kv_columns, kv_columns, 1)
    positions = (lengths[:, None] + jnp.arange(STEPS, dtype=jnp.int32)[None, :]).astype(jnp.float32)
    half = HEAD // 2
    frequency = 10000.0 ** (-(jnp.arange(half, dtype=jnp.float32) * 2.0 / HEAD))
    angles = positions[..., None] * frequency

    def table(values):
        per_head = jnp.repeat(values, heads_local, axis=1)
        filler = jnp.zeros((req_local, 24 - STEPS - STEPS * heads_local, half), jnp.float32)
        return jnp.concatenate([per_head, values, filler], 1)

    cosine, sine = table(jnp.cos(angles)), table(jnp.sin(angles))

    peers = gx_count * gy_count * req_local // block_requests
    sent = gather_and_project(tokens.reshape(rows, depth), q_weight, own_kv, peers)
    everywhere = ("gx", "gy")
    sent = sent.reshape(gx_count * gy_count, req_local * MESSAGE, LANES)
    partials = lax.all_to_all(sent, everywhere, split_axis=0, concat_axis=0, tiled=True)
    partials = partials.reshape(gx_count, gy_count, req_local * MESSAGE, LANES)
    attended = attend(lengths, partials, cosine, sine, kv_cache)
    attended = attended.reshape(gx_count * gy_count, req_local * REPLY, LANES)
    attended = lax.all_to_all(attended, everywhere, split_axis=0, concat_axis=0, tiled=True)
    attended = attended.reshape(-1, LANES)

    shifts = jnp.arange(ring, dtype=jnp.int32)
    ahead = (y + shifts) % ring * 2
    for_other = output_partial(ahead + 1 - core, attended, out_weight, rows)
    from_other = move(for_other, 0, 1)
    mine = output_partial(ahead + core, attended, out_weight, rows)
    mine = plus(mine, from_other)
    cut = rows // 2
    front = move(mine[2, :cut], 1, 0)
    back = move(mine[2, cut:], -1, 0)
    up = jnp.concatenate([plus(mine[1, :cut], front), mine[1, cut:]], 0)
    down = jnp.concatenate([mine[3, :cut], plus(mine[3, cut:], back)], 0)
    from_below = move(up, 1, 0)
    from_above = move(down, -1, 0)
    result = (
        mine[0].astype(jnp.float32)
        + from_below.astype(jnp.float32)
        + from_above.astype(jnp.float32)
    ).astype(jnp.bfloat16)
    return result.reshape(steps, block_requests, -1)


def solution(mesh):
    in_specs = (
        P(None, "gy", "gx"),
        P("gx", "gy"),
        P("gx", None),
        P("gy", "gx"),
        P(("gx", "gy"), None, None),
        P(("gx", "gy")),
    )
    out_specs = P(None, "gy", "gx")
    return jax.shard_map(
        per_device, mesh=mesh, in_specs=in_specs, out_specs=out_specs, check_vma=False
    )
```

time: 161 us -> 146 us (0.907)
  starting transfers between devices: 34.2 us -> 26.7 us
  waiting for transfers between devices: 87.9 us -> 82.7 us
  Pallas kernels: 31.4 us -> 28.1 us
  local copies, waits for them, and re-layouts: 2.48 us -> 4.35 us
    pallas_call x2, Pallas kernels: 12 us -> 5.01 us  [output_partial(): pl.pallas_call(output_kernel, out_shape=jax.ShapeDtypeStruct((blocks, row...]
    all_to_all x1, starting transfers between devices: 9.44 us -> 4.85 us  [per_device(): lax.all_to_all(attended, everywhere, split_axis=0, concat_axis=0, tiled=T...]
    pallas_call x2 -> x3, Pallas kernels: 19.5 us -> 23 us  [the longest x1 12.1 us: attend(): pl.pallas_call(attend_kernel, out_shape=jax.ShapeDtypeStruct((peers, repl...]
    ppermute x13, waiting for transfers between devices: 18.1 us -> 15 us  [move(): return lax.ppermute(value, 'gy', across(step_y, step_core))]
    all_to_all x1, starting transfers between devices: 12.1 us -> 9.13 us  [per_device(): lax.all_to_all(sent, everywhere, split_axis=0, concat_axis=0, tiled=True)]
    unnamed x19 -> x20, local copies, waits for them, and re-layouts: 0.86 us -> 3.41 us
    all_to_all x1, waiting for transfers between devices: 35.2 us -> 33.1 us  [per_device(): lax.all_to_all(attended, everywhere, split_axis=0, concat_axis=0, tiled=T...]
  transfers between devices with their start and end apart: 15 -> 15, of which waited for: 9 -> 7; matrix products, arithmetic and copies ran while one was open for 2% -> 2% of each run, Pallas kernels for 4% -> 5%
where the time goes in v2:
time: 146 us; the launch traced here: 145 us
  waiting for transfers between devices  82.7 us (57%)
  Pallas kernels  28.1 us (19%)
  starting transfers between devices  26.7 us (18%)
  local copies, waits for them, and re-layouts  4.35 us (3%)
  other arithmetic  3.24 us (2%)
    all_to_all x1, waiting for transfers between devices, per_device(): lax.all_to_all(sent, everywhere, split_axis=0, concat_axis=0, tiled=True)  34.6 us
    all_to_all x1, waiting for transfers between devices, per_device(): lax.all_to_all(attended, everywhere, split_axis=0, concat_axis=0, tiled=T...  33.1 us
    ppermute x13, waiting for transfers between devices, move(): return lax.ppermute(value, 'gy', across(step_y, step_core))  15 us
    ppermute x13, starting transfers between devices, move(): return lax.ppermute(value, 'gy', across(step_y, step_core))  12.8 us
    pallas_call x1, Pallas kernels, attend(): pl.pallas_call(attend_kernel, out_shape=jax.ShapeDtypeStruct((peers, repl...  12.1 us
    pallas_call x2, Pallas kernels, project(): pl.pallas_call(functools.partial(project_kernel, count), out_shape=jax.Sh...  10.9 us
    all_to_all x1, starting transfers between devices, per_device(): lax.all_to_all(sent, everywhere, split_axis=0, concat_axis=0, tiled=True)  9.13 us
    pallas_call x2, Pallas kernels, output_partial(): pl.pallas_call(output_kernel, out_shape=jax.ShapeDtypeStruct((blocks, row...  5.01 us
  transfers between devices with their start and end apart: 15, of which 7 were waited for; matrix products, arithmetic and copies ran while one was open for 2% of the time, Pallas kernels for 5%

profile of v2, /device:TPU:0, one launch (start us, length us, event | category | flops | bytes accessed | tf_op | source)
XLA Modules:
  0.0 145.4 jit_solution(11988012431310131251)
XLA Ops:
  0.0 1.7 %collective-permute-start = (bf16[96,1152]{1,0:T(8,128)(2,1)}, bf16[96,1152]{1,0:T(8,128)(2,1)S(1)}, u32[]{:S(2)}, u32[]{:S(2)}) collective-permute-start(bf16[96,1152]{1,0:T(8,128)(2,1)} %bitcast.43), channel_id=1, source_target_pairs={{0,2},{1,3},{2,4},{3,5},{4,6},{5,7},{6,0},{7,1},{8,10},{9,11},{10,... | collective-permute-start | bytes 663560 | tf_op jit(solution)/shard_map/ppermute | solution.py:32
  1.7 1.6 %collective-permute-start.2 = (bf16[96,1152]{1,0:T(8,128)(2,1)}, bf16[96,1152]{1,0:T(8,128)(2,1)S(1)}, u32[]{:S(2)}, u32[]{:S(2)}) collective-permute-start(bf16[96,1152]{1,0:T(8,128)(2,1)} %bitcast.44), channel_id=1, source_target_pairs={{0,6},{1,7},{2,0},{3,1},{4,2},{5,3},{6,4},{7,5},{8,14},{9,15},{10,... | collective-permute-start | bytes 663560 | tf_op jit(solution)/shard_map/ppermute | solution.py:32
  3.2 0.0 collective-permute-start.6
  3.2 0.8 constant_dynamic-slice_fusion.refs_5_
  4.0 4.7 %collective-permute-done.refs_2_ = bf16[96,1152]{1,0:T(8,128)(2,1)S(1)} collective-permute-done((bf16[96,1152]{1,0:T(8,128)(2,1)}, bf16[96,1152]{1,0:T(8,128)(2,1)S(1)}, u32[]{:S(2)}, u32[]{:S(2)}) %collective-permute-start) | collective-permute-done | bytes 221216 | tf_op jit(solution)/shard_map/ppermute | solution.py:32
  8.8 0.4 collective-permute-start.4
  9.1 0.0 collective-permute-done.2.refs_3_
  9.1 3.0 %collective-permute-start.5 = (bf16[48,1152]{1,0:T(8,128)(2,1)S(1)}, bf16[48,1152]{1,0:T(8,128)(2,1)S(1)}, u32[]{:S(2)}, u32[]{:S(2)}) collective-permute-start(bf16[48,1152]{1,0:T(8,128)(2,1)S(1)} %slice.37), channel_id=1, source_target_pairs={{0,6},{1,7},{2,0},{3,1},{4,2},{5,3},{6,4},{7,5},{8,14},{9,15},{10,... | collective-permute-start | bytes 331784 | tf_op jit(solution)/shard_map/ppermute | solution.py:32
  12.1 0.6 pad_add_fusion.1.places
  12.7 0.0 collective-permute-start.1
  12.7 0.5 collective-permute-start.3
  13.2 0.0 collective-permute-done.6.refs_1_
  13.2 0.0 copy-start.8
  13.2 0.7 copy-done.8
  13.9 5.5 %project.2.refs_6_ = bf16[10240,128]{1,0:T(8,128)(2,1)} custom-call(s32[4]{0:T(128)} %pad_add_fusion.1.places, bf16[96,1152]{1,0:T(8,128)(2,1)} %bitcast.46, bf16[96,1152]{1,0:T(8,128)(2,1)} %copy-done.8, bf16[96,1152]{1,0:T(8,128)(2,1)} %copy-done.3, bf16[96,1152]{1,0:T(8,128)(2,1)} %copy-done.4, bf16[1152,1536]{1,0:T(8,128)(2,1)} %refs_4_.3, ...), custom_call_target="tpu_custom_call" | custom-call | tf_op jit(solution)/shard_map/project/pallas_call | solution.py:115
  19.4 0.0 collective-permute-done.5
  19.4 0.1 collective-permute-start.7
  19.6 0.7 pad_add_fusion.places
  20.2 0.0 collective-permute-done.1.refs_0_
  20.2 0.0 collective-permute-done.3.refs_1_
  20.2 0.8 collective-permute-done.7.refs_3_
  21.0 0.7 copy-done.7
  21.7 5.5 %project.3 = bf16[10240,128]{1,0:T(8,128)(2,1)} custom-call(s32[4]{0:T(128)} %pad_add_fusion.places, bf16[96,1152]{1,0:T(8,128)(2,1)} %copy-done.5, bf16[96,1152]{1,0:T(8,128)(2,1)} %copy-done.6, bf16[96,1152]{1,0:T(8,128)(2,1)} %copy-done.2, bf16[96,1152]{1,0:T(8,128)(2,1)} %copy-done.7, ...), custom_call_target="tpu_custom_call", output_to_operand_aliasing={{}: (7, {})} | custom-call | tf_op jit(solution)/shard_map/project/pallas_call | solution.py:115
  27.2 0.0 copy-start.9
  27.2 9.1 %all-to-all-start = ((bf16[128,80,128]{2,1,0:T(8,128)(2,1)}), bf16[128,80,128]{2,1,0:T(8,128)(2,1)}, u32[]{:S(2)}, u32[]{:S(2)}) async-start(bf16[128,80,128]{2,1,0:T(8,128)(2,1)} %bitcast.41), calls=%async_computation | async-start | bytes 5242880 | tf_op jit(solution)/shard_map/all_to_all | solution.py:375
  36.4 0.1 add_convert_fusion.1
  36.4 0.1 multiply_sine_fusion
  36.6 0.1 pad.9.clone
  36.7 0.7 maximum_maximum_fusion.1
  37.4 34.6 %all-to-all-done = bf16[128,80,128]{2,1,0:T(8,128)(2,1)} async-done(((bf16[128,80,128]{2,1,0:T(8,128)(2,1)}), bf16[128,80,128]{2,1,0:T(8,128)(2,1)}, u32[]{:S(2)}, u32[]{:S(2)}) %all-to-all-start) | async-done | bytes 2621472 | tf_op jit(solution)/shard_map/all_to_all | solution.py:375
  72.1 12.1 %attend.1 = bf16[16,576,128]{2,1,0:T(8,128)(2,1)} custom-call(s32[2]{0:T(128)} %lengths.1, bf16[16,8,80,128]{3,2,1,0:T(8,128)(2,1)} %bitcast.10.partials, f32[2,24,128]{2,1,0:T(8,128)} %get-tuple-element.18.cosine, f32[2,24,128]{2,1,0:T(8,128)} %get-tuple-element.17.sine, bf16[2,8192,512]{2,1,0:T(8,128)(2,1)} %cache.1), custom_call_target="tpu_custom_call" | custom-call | tf_op jit(solution)/shard_map/attend/pallas_call | solution.py:279
  84.2 4.9 %all-to-all-start.1 = ((bf16[128,72,128]{2,1,0:T(8,128)(2,1)}), bf16[128,72,128]{2,1,0:T(8,128)(2,1)S(1)}, u32[]{:S(2)}, u32[]{:S(2)}) async-start(bf16[128,72,128]{2,1,0:T(8,128)(2,1)} %bitcast.42), calls=%async_computation.1 | async-start | bytes 4718592 | tf_op jit(solution)/shard_map/all_to_all | solution.py:379
  89.0 33.1 %all-to-all-done.1 = bf16[128,72,128]{2,1,0:T(8,128)(2,1)S(1)} async-done(((bf16[128,72,128]{2,1,0:T(8,128)(2,1)}), bf16[128,72,128]{2,1,0:T(8,128)(2,1)S(1)}, u32[]{:S(2)}, u32[]{:S(2)}) %all-to-all-start.1) | async-done | bytes 2359328 | tf_op jit(solution)/shard_map/all_to_all | solution.py:379
  122.1 2.0 %copy-done.1 = bf16[1536,1152]{1,0:T(8,128)(2,1)S(1)} copy-done((bf16[1536,1152]{1,0:T(8,128)(2,1)S(1)}, bf16[1536,1152]{1,0:T(8,128)(2,1)}, u32[]{:S(2)}) %copy-start.1) | copy-done | bytes 3538968
  124.1 2.5 %output.3 = bf16[4,96,1152]{2,1,0:T(8,128)(2,1)S(1)} custom-call(s32[4]{0:T(128)S(1)} %add_subtract_fusion.places, bf16[9216,128]{1,0:T(8,128)(2,1)S(1)} %bitcast.39, bf16[1536,1152]{1,0:T(8,128)(2,1)S(1)} %copy-done.1), custom_call_target="tpu_custom_call" | custom-call | tf_op jit(solution)/shard_map/output/pallas_call | solution.py:329
  126.6 0.1 collective-permute-start.8
  126.7 2.5 %output.2 = bf16[4,96,1152]{2,1,0:T(8,128)(2,1)S(1)} custom-call(s32[4]{0:T(128)S(1)} %broadcast_add_fusion.places, bf16[9216,128]{1,0:T(8,128)(2,1)S(1)} %bitcast.40, bf16[1536,1152]{1,0:T(8,128)(2,1)S(1)} %copy-done.1), custom_call_target="tpu_custom_call" | custom-call | tf_op jit(solution)/shard_map/output/pallas_call | solution.py:329
  129.2 0.0 collective-permute-done.8
  129.3 0.2 add_convert_fusion
  129.5 0.6 collective-permute-start.11
  130.1 1.5 %collective-permute-start.9 = (bf16[48,1152]{1,0:T(8,128)(2,1)S(1)}, bf16[48,1152]{1,0:T(8,128)(2,1)S(1)}, u32[]{:S(2)}, u32[]{:S(2)}) collective-permute-start(bf16[48,1152]{1,0:T(8,128)(2,1)S(1)} %get-tuple-element.11), channel_id=1, source_target_pairs={{0,2},{1,3},{2,4},{3,5},{4,6},{5,7},{6,0},{7,1},{8,10},{9,11},{10,... | collective-permute-start | bytes 331784 | tf_op jit(solution)/shard_map/ppermute | solution.py:32
  131.6 3.4 %collective-permute-done.11 = bf16[48,1152]{1,0:T(8,128)(2,1)S(1)} collective-permute-done((bf16[48,1152]{1,0:T(8,128)(2,1)S(1)}, bf16[48,1152]{1,0:T(8,128)(2,1)S(1)}, u32[]{:S(2)}, u32[]{:S(2)}) %collective-permute-start.11) | collective-permute-done | bytes 110624 | tf_op jit(solution)/shard_map/ppermute | solution.py:32
  135.0 1.5 %collective-permute-done.9 = bf16[48,1152]{1,0:T(8,128)(2,1)S(1)} collective-permute-done((bf16[48,1152]{1,0:T(8,128)(2,1)S(1)}, bf16[48,1152]{1,0:T(8,128)(2,1)S(1)}, u32[]{:S(2)}, u32[]{:S(2)}) %collective-permute-start.9) | collective-permute-done | bytes 110624 | tf_op jit(solution)/shard_map/ppermute | solution.py:32
  136.5 0.1 fusion.3
  136.6 0.4 collective-permute-start.10
  137.0 3.0 %collective-permute-start.12 = (bf16[96,1152]{1,0:T(8,128)(2,1)S(1)}, bf16[96,1152]{1,0:T(8,128)(2,1)S(1)}, u32[]{:S(2)}, u32[]{:S(2)}) collective-permute-start(bf16[96,1152]{1,0:T(8,128)(2,1)S(1)} %pad_maximum_fusion.2), channel_id=1, source_target_pairs={{0,6},{1,7},{2,0},{3,1},{4,2},{5,3},{6,4},{7,5},{8,14},{9,15},{10,... | collective-permute-start | bytes 663560 | tf_op jit(solution)/shard_map/ppermute | solution.py:32
  140.0 4.6 %collective-permute-done.10 = bf16[96,1152]{1,0:T(8,128)(2,1)S(1)} collective-permute-done((bf16[96,1152]{1,0:T(8,128)(2,1)S(1)}, bf16[96,1152]{1,0:T(8,128)(2,1)S(1)}, u32[]{:S(2)}, u32[]{:S(2)}) %collective-permute-start.10) | collective-permute-done | bytes 221216 | tf_op jit(solution)/shard_map/ppermute | solution.py:32
  144.6 0.8 fusion.1
  (33 shorter events, 0.2 us)
Async XLA Ops:
  0.0 3.2 %copy-start = (bf16[1152,512]{1,0:T(8,128)(2,1)S(1)}, bf16[1152,512]{1,0:T(8,128)(2,1)}, u32[]{:S(2)}) copy-start(bf16[1152,512]{1,0:T(8,128)(2,1)} %param.8) | copy-start | bytes 3538948
  0.0 8.7 %collective-permute-start = (bf16[96,1152]{1,0:T(8,128)(2,1)}, bf16[96,1152]{1,0:T(8,128)(2,1)S(1)}, u32[]{:S(2)}, u32[]{:S(2)}) collective-permute-start(bf16[96,1152]{1,0:T(8,128)(2,1)} %bitcast.43), channel_id=1, source_target_pairs={{0,2},{1,3},{2,4},{3,5},{4,6},{5,7},{6,0},{7,1},{8,10},{9,11},{10,... | collective-permute-start | bytes 663560 | tf_op jit(solution)/shard_map/ppermute | solution.py:32
  1.7 7.5 %collective-permute-start.2 = (bf16[96,1152]{1,0:T(8,128)(2,1)}, bf16[96,1152]{1,0:T(8,128)(2,1)S(1)}, u32[]{:S(2)}, u32[]{:S(2)}) collective-permute-start(bf16[96,1152]{1,0:T(8,128)(2,1)} %bitcast.44), channel_id=1, source_target_pairs={{0,6},{1,7},{2,0},{3,1},{4,2},{5,3},{6,4},{7,5},{8,14},{9,15},{10,... | collective-permute-start | bytes 663560 | tf_op jit(solution)/shard_map/ppermute | solution.py:32
  3.2 10.0 %collective-permute-start.6 = (bf16[96,1152]{1,0:T(8,128)(2,1)}, bf16[96,1152]{1,0:T(8,128)(2,1)S(1)}, u32[]{:S(2)}, u32[]{:S(2)}) collective-permute-start(bf16[96,1152]{1,0:T(8,128)(2,1)} %bitcast.45), channel_id=1, source_target_pairs={{0,1},{1,0},{2,3},{3,2},{4,5},{5,4},{6,7},{7,6},{8,9},{9,8},{10,11... | collective-permute-start | bytes 663560 | tf_op jit(solution)/shard_map/ppermute | solution.py:32
  8.7 4.5 %copy-start.3 = (bf16[96,1152]{1,0:T(8,128)(2,1)}, bf16[96,1152]{1,0:T(8,128)(2,1)S(1)}, u32[]{:S(2)}) copy-start(bf16[96,1152]{1,0:T(8,128)(2,1)S(1)} %collective-permute-done.refs_2_) | copy-start | bytes 663556
  8.8 10.6 %collective-permute-start.4 = (bf16[48,1152]{1,0:T(8,128)(2,1)S(1)}, bf16[48,1152]{1,0:T(8,128)(2,1)S(1)}, u32[]{:S(2)}, u32[]{:S(2)}) collective-permute-start(bf16[48,1152]{1,0:T(8,128)(2,1)S(1)} %slice.36), channel_id=1, source_target_pairs={{0,2},{1,3},{2,4},{3,5},{4,6},{5,7},{6,0},{7,1},{8,10},{9,11},{10,... | collective-permute-start | bytes 331784 | tf_op jit(solution)/shard_map/ppermute | solution.py:32
  9.1 4.1 %copy-start.4 = (bf16[96,1152]{1,0:T(8,128)(2,1)}, bf16[96,1152]{1,0:T(8,128)(2,1)S(1)}, u32[]{:S(2)}) copy-start(bf16[96,1152]{1,0:T(8,128)(2,1)S(1)} %collective-permute-done.2.refs_3_) | copy-start | bytes 663556
  9.1 10.3 %collective-permute-start.5 = (bf16[48,1152]{1,0:T(8,128)(2,1)S(1)}, bf16[48,1152]{1,0:T(8,128)(2,1)S(1)}, u32[]{:S(2)}, u32[]{:S(2)}) collective-permute-start(bf16[48,1152]{1,0:T(8,128)(2,1)S(1)} %slice.37), channel_id=1, source_target_pairs={{0,6},{1,7},{2,0},{3,1},{4,2},{5,3},{6,4},{7,5},{8,14},{9,15},{10,... | collective-permute-start | bytes 331784 | tf_op jit(solution)/shard_map/ppermute | solution.py:32
  12.7 7.5 %collective-permute-start.1 = (bf16[96,1152]{1,0:T(8,128)(2,1)S(1)}, bf16[96,1152]{1,0:T(8,128)(2,1)S(1)}, u32[]{:S(2)}, u32[]{:S(2)}) collective-permute-start(bf16[96,1152]{1,0:T(8,128)(2,1)S(1)} %collective-permute-done.refs_2_), channel_id=1, source_target_pairs={{0,1},{1,0},{2,3},{3,2},{4,5},{5,4},{6,7},{7,6},{8,9},{9,8},{10,11... | collective-permute-start | bytes 663560 | tf_op jit(solution)/shard_map/ppermute | solution.py:32
  12.7 7.5 %collective-permute-start.3 = (bf16[96,1152]{1,0:T(8,128)(2,1)S(1)}, bf16[96,1152]{1,0:T(8,128)(2,1)S(1)}, u32[]{:S(2)}, u32[]{:S(2)}) collective-permute-start(bf16[96,1152]{1,0:T(8,128)(2,1)S(1)} %collective-permute-done.2.refs_3_), channel_id=1, source_target_pairs={{0,1},{1,0},{2,3},{3,2},{4,5},{5,4},{6,7},{7,6},{8,9},{9,8},{10,11... | collective-permute-start | bytes 663560 | tf_op jit(solution)/shard_map/ppermute | solution.py:32
  13.2 0.7 copy-start.8
  19.4 1.6 %copy-start.2 = (bf16[96,1152]{1,0:T(8,128)(2,1)}, bf16[96,1152]{1,0:T(8,128)(2,1)S(1)}, u32[]{:S(2)}) copy-start(bf16[96,1152]{1,0:T(8,128)(2,1)S(1)} %pad_maximum_fusion.refs_2_) | copy-start | bytes 663556
  19.4 1.6 %collective-permute-start.7 = (bf16[96,1152]{1,0:T(8,128)(2,1)S(1)}, bf16[96,1152]{1,0:T(8,128)(2,1)S(1)}, u32[]{:S(2)}, u32[]{:S(2)}) collective-permute-start(bf16[96,1152]{1,0:T(8,128)(2,1)S(1)} %pad_maximum_fusion.refs_2_), channel_id=1, source_target_pairs={{0,1},{1,0},{2,3},{3,2},{4,5},{5,4},{6,7},{7,6},{8,9},{9,8},{10,11... | collective-permute-start | bytes 663560 | tf_op jit(solution)/shard_map/ppermute | solution.py:32
  20.2 0.8 copy-start.5
  20.2 0.8 copy-start.6
  21.0 0.7 copy-start.7
  27.2 9.2 %copy-start.9 = (s32[2]{0:T(128)S(1)}, s32[2]{0:T(128)}, u32[]{:S(2)}) copy-start(s32[2]{0:T(128)} %lengths.1) | copy-start | bytes 28
  27.2 44.8 %all-to-all-start = ((bf16[128,80,128]{2,1,0:T(8,128)(2,1)}), bf16[128,80,128]{2,1,0:T(8,128)(2,1)}, u32[]{:S(2)}, u32[]{:S(2)}) async-start(bf16[128,80,128]{2,1,0:T(8,128)(2,1)} %bitcast.41), calls=%async_computation | async-start | bytes 5242880 | tf_op jit(solution)/shard_map/all_to_all | solution.py:375
  84.2 37.9 %all-to-all-start.1 = ((bf16[128,72,128]{2,1,0:T(8,128)(2,1)}), bf16[128,72,128]{2,1,0:T(8,128)(2,1)S(1)}, u32[]{:S(2)}, u32[]{:S(2)}) async-start(bf16[128,72,128]{2,1,0:T(8,128)(2,1)} %bitcast.42), calls=%async_computation.1 | async-start | bytes 4718592 | tf_op jit(solution)/shard_map/all_to_all | solution.py:379
  122.1 2.0 %copy-start.1 = (bf16[1536,1152]{1,0:T(8,128)(2,1)S(1)}, bf16[1536,1152]{1,0:T(8,128)(2,1)}, u32[]{:S(2)}) copy-start(bf16[1536,1152]{1,0:T(8,128)(2,1)} %out_weight.3) | copy-start | bytes 10616836
  126.6 2.6 %collective-permute-start.8 = (bf16[4,96,1152]{2,1,0:T(8,128)(2,1)S(1)}, bf16[4,96,1152]{2,1,0:T(8,128)(2,1)S(1)}, u32[]{:S(2)}, u32[]{:S(2)}) collective-permute-start(bf16[4,96,1152]{2,1,0:T(8,128)(2,1)S(1)} %output.3), channel_id=1, source_target_pairs={{0,1},{1,0},{2,3},{3,2},{4,5},{5,4},{6,7},{7,6},{8,9},{9,8},{10,11... | collective-permute-start | bytes 2654216 | tf_op jit(solution)/shard_map/ppermute | solution.py:32
  129.5 5.5 %collective-permute-start.11 = (bf16[48,1152]{1,0:T(8,128)(2,1)S(1)}, bf16[48,1152]{1,0:T(8,128)(2,1)S(1)}, u32[]{:S(2)}, u32[]{:S(2)}) collective-permute-start(bf16[48,1152]{1,0:T(8,128)(2,1)S(1)} %get-tuple-element.12), channel_id=1, source_target_pairs={{0,6},{1,7},{2,0},{3,1},{4,2},{5,3},{6,4},{7,5},{8,14},{9,15},{10,... | collective-permute-start | bytes 331784 | tf_op jit(solution)/shard_map/ppermute | solution.py:32
  130.1 6.4 %collective-permute-start.9 = (bf16[48,1152]{1,0:T(8,128)(2,1)S(1)}, bf16[48,1152]{1,0:T(8,128)(2,1)S(1)}, u32[]{:S(2)}, u32[]{:S(2)}) collective-permute-start(bf16[48,1152]{1,0:T(8,128)(2,1)S(1)} %get-tuple-element.11), channel_id=1, source_target_pairs={{0,2},{1,3},{2,4},{3,5},{4,6},{5,7},{6,0},{7,1},{8,10},{9,11},{10,... | collective-permute-start | bytes 331784 | tf_op jit(solution)/shard_map/ppermute | solution.py:32
  136.6 8.0 %collective-permute-start.10 = (bf16[96,1152]{1,0:T(8,128)(2,1)S(1)}, bf16[96,1152]{1,0:T(8,128)(2,1)S(1)}, u32[]{:S(2)}, u32[]{:S(2)}) collective-permute-start(bf16[96,1152]{1,0:T(8,128)(2,1)S(1)} %pad_maximum_fusion.1), channel_id=1, source_target_pairs={{0,2},{1,3},{2,4},{3,5},{4,6},{5,7},{6,0},{7,1},{8,10},{9,11},{10,... | collective-permute-start | bytes 663560 | tf_op jit(solution)/shard_map/ppermute | solution.py:32
  137.0 7.6 %collective-permute-start.12 = (bf16[96,1152]{1,0:T(8,128)(2,1)S(1)}, bf16[96,1152]{1,0:T(8,128)(2,1)S(1)}, u32[]{:S(2)}, u32[]{:S(2)}) collective-permute-start(bf16[96,1152]{1,0:T(8,128)(2,1)S(1)} %pad_maximum_fusion.2), channel_id=1, source_target_pairs={{0,6},{1,7},{2,0},{3,1},{4,2},{5,3},{6,4},{7,5},{8,14},{9,15},{10,... | collective-permute-start | bytes 663560 | tf_op jit(solution)/shard_map/ppermute | solution.py:32

commit v3 on v2

--- a/solution.py
+++ b/solution.py
@@ -14,7 +14,7 @@
 MESSAGE = 40
 REPLY = 36
 LOG2_E = 1.4426950408889634
-PROJECT_VMEM = 56 * 1024 * 1024
+PROJECT_VMEM = 53 * 1024 * 1024
 ATTEND_VMEM = 60 * 1024 * 1024
 OUTPUT_VMEM = 24 * 1024 * 1024
 
@@ -130,8 +130,8 @@
 
 
 def attend_kernel(
-    lengths, partials, cosine, sine, cache, out, keys, values, summed, query, replies, narrow, score,
-    arrived, sent
+    lengths, partials, cosine, sine, cached_keys, cache, out, keys, values, summed, query, replies, narrow,
+    score, arrived, sent
 ):
     peers, group, _, _ = partials.shape
     requests, slots, _ = cache.shape
@@ -142,11 +142,12 @@
 
     def fetch(request, side, block):
         place = pl.ds(pl.multiple_of(block * SLOT_BLOCK, SLOT_BLOCK), SLOT_BLOCK)
-        return pltpu.make_async_copy(
-            cache.at[request, place, pl.ds(side * HEAD, HEAD)],
-            (keys, values)[side].at[request, place],
-            arrived.at[request, side, block],
-        )
+        if side == 0:
+            source, target = cached_keys.at[request, :, place], keys.at[request, :, place]
+        else:
+            source = cache.at[request, place, pl.ds(HEAD, HEAD)]
+            target = values.at[request, place]
+        return pltpu.make_async_copy(source, target, arrived.at[request, side, block])
 
     def start(request, side):
         if request < requests:
@@ -160,7 +161,6 @@
             total = total + partials[peer, place].astype(jnp.float32)
         summed[place] = total.astype(jnp.bfloat16).astype(jnp.float32)
 
-    start(1, 0)
     start(0, 1)
     row_step = lax.broadcasted_iota(jnp.int32, (rows, LANES), 0) % heads_rows // (heads_rows // STEPS)
     column = lax.broadcasted_iota(jnp.int32, (rows, LANES), 1)
@@ -197,8 +197,8 @@
         fetch(request, 0, block).wait()
         slot = block * SLOT_BLOCK + lax.broadcasted_iota(jnp.int32, (1, SLOT_BLOCK), 1)
         hidden = jnp.where(slot < lengths[request], jnp.float32(0.0), jnp.float32(-1e30))
-        scores = hidden + lax.dot_general(
-            queries, keys[request, place], (((1,), (1,)), ((), ())), preferred_element_type=jnp.float32
+        scores = hidden + jnp.dot(
+            queries, keys[request, :, place], preferred_element_type=jnp.float32
         )
         score[request, block] = scores
         for lane in range(0, SLOT_BLOCK, LANES):
@@ -231,33 +231,19 @@
             replies[base + heads_rows : base + 2 * heads_rows] = query[request, source, LANES:]
 
     ready = [prepare(request) for request in range(requests)]
-    queries, new_scores, _ = ready[0]
-    top = lax.fori_loop(
-        0, blocks, functools.partial(score_block, 0, queries), new_scores
-    )
     for request in range(requests):
-        _, new_scores, new_values = ready[request]
+        queries, new_scores, new_values = ready[request]
+        start(request + 1, 0)
+        top = lax.fori_loop(
+            0, blocks, functools.partial(score_block, request, queries), new_scores
+        )
+        start(request + 1, 1)
         top, denom, accum = begin(new_scores, new_values, top)
-        start(request + 1, 1)
-        start(request + 2, 0)
-        if request + 1 < requests:
-            following, following_scores, _ = ready[request + 1]
-
-            def both(block, state, request=request, top=top, following=following):
-                next_top, denom, accum = state
-                next_top = score_block(request + 1, following, block, next_top)
-                denom, accum = mix_block(request, top, block, denom, accum)
-                return next_top, denom, accum
-
-            top, denom, accum = lax.fori_loop(
-                0, blocks, both, (following_scores, denom, accum)
-            )
-        else:
-
-            def last(block, state, request=request, top=top):
-                return mix_block(request, top, block, *state)
-
-            denom, accum = lax.fori_loop(0, blocks, last, (denom, accum))
+
+        def mix(block, state, request=request, top=top):
+            return mix_block(request, top, block, *state)
+
+        denom, accum = lax.fori_loop(0, blocks, mix, (denom, accum))
         finish(request, denom, accum)
 
     narrow[...] = replies[...].astype(jnp.bfloat16)
@@ -268,7 +254,7 @@
         copy.wait()
 
 
-def attend(lengths, partials, cosine, sine, cache):
+def attend(lengths, partials, cosine, sine, cached_keys, cache):
     peers, group, rows, _ = partials.shape
     requests, slots, _ = cache.shape
     blocks = slots // SLOT_BLOCK
@@ -279,10 +265,10 @@
     return pl.pallas_call(
         attend_kernel,
         out_shape=jax.ShapeDtypeStruct((peers, reply_rows, LANES), jnp.bfloat16),
-        in_specs=[pl.BlockSpec(memory_space=pltpu.SMEM), vmem, vmem, vmem, hbm],
+        in_specs=[pl.BlockSpec(memory_space=pltpu.SMEM), vmem, vmem, vmem, hbm, hbm],
         out_specs=hbm,
         scratch_shapes=[
-            pltpu.VMEM((requests, slots, HEAD), jnp.bfloat16),
+            pltpu.VMEM((requests, HEAD, slots), jnp.bfloat16),
             pltpu.VMEM((requests, slots, HEAD), jnp.bfloat16),
             pltpu.VMEM((group, rows, LANES), jnp.float32),
             pltpu.VMEM((requests, query_rows, HEAD), jnp.float32),
@@ -294,14 +280,15 @@
         ],
         compiler_params=pltpu.CompilerParams(vmem_limit_bytes=ATTEND_VMEM),
         name="attend",
-    )(lengths, partials, cosine, sine, cache)
-
-
-def output_kernel(places, attended, out_weight, out, spread, rows_ref):
-    blocks, rows, width = out.shape
-    requests = rows // STEPS
-    heads = out_weight.shape[0] // HEAD
-    size = requests * REPLY
+    )(lengths, partials, cosine, sine, cached_keys, cache)
+
+
+def arrange_kernel(places, attended, out, spread):
+    blocks = places.shape[0]
+    size = spread.shape[0]
+    requests = size // REPLY
+    rows = requests * STEPS
+    heads = out.shape[1] // HEAD
     for index in range(blocks):
         first = pl.multiple_of(places[index] * size, size)
         spread[...] = attended[pl.ds(first, size), :].astype(jnp.float32)
@@ -311,33 +298,47 @@
                     spot = side * STEPS * heads + step * heads + head
                     lane = head * HEAD + side * LANES
                     start = index * rows + step * requests
-                    rows_ref[start : start + requests, lane : lane + LANES] = spread[
+                    out[start : start + requests, lane : lane + LANES] = spread[
                         pl.ds(spot, requests, stride=REPLY), :
                     ].astype(jnp.bfloat16)
+
+
+def arrange(places, attended, rows, depth):
+    vmem = pl.BlockSpec(memory_space=pltpu.VMEM)
+    return pl.pallas_call(
+        arrange_kernel,
+        out_shape=jax.ShapeDtypeStruct((places.shape[0] * rows, depth), jnp.bfloat16),
+        in_specs=[pl.BlockSpec(memory_space=pltpu.SMEM), vmem],
+        out_specs=vmem,
+        scratch_shapes=[pltpu.VMEM((rows // STEPS * REPLY, LANES), jnp.float32)],
+        compiler_params=pltpu.CompilerParams(vmem_limit_bytes=OUTPUT_VMEM),
+        name="arrange",
+    )(places, attended)
+
+
+def output_kernel(half, arranged, out_weight, out):
+    blocks, rows, width = out.shape
+    taken = pl.ds(half * blocks * rows, blocks * rows)
     for first in range(0, width, HEAD):
         size = min(HEAD, width - first)
         partial = jnp.dot(
-            rows_ref[...], out_weight[:, first : first + size], preferred_element_type=jnp.float32
+            arranged[taken, :], out_weight[:, first : first + size], preferred_element_type=jnp.float32
         ).astype(jnp.bfloat16)
         for index in range(blocks):
             out[index, :, first : first + size] = partial[index * rows : (index + 1) * rows]
 
 
-def output_partial(places, attended, out_weight, rows):
-    blocks = places.shape[0]
+def output_partial(half, arranged, out_weight, rows):
+    blocks = arranged.shape[0] // rows // 2
     vmem = pl.BlockSpec(memory_space=pltpu.VMEM)
     return pl.pallas_call(
-        output_kernel,
+        functools.partial(output_kernel, half),
         out_shape=jax.ShapeDtypeStruct((blocks, rows, out_weight.shape[1]), jnp.bfloat16),
-        in_specs=[pl.BlockSpec(memory_space=pltpu.SMEM), vmem, vmem],
+        in_specs=[vmem, vmem],
         out_specs=vmem,
-        scratch_shapes=[
-            pltpu.VMEM((rows // STEPS * REPLY, LANES), jnp.float32),
-            pltpu.VMEM((blocks * rows, out_weight.shape[0]), jnp.bfloat16),
-        ],
         compiler_params=pltpu.CompilerParams(vmem_limit_bytes=OUTPUT_VMEM),
         name="output",
-    )(places, attended, out_weight)
+    )(arranged, out_weight)
 
 
 def plus(first, second):
@@ -374,29 +375,28 @@
     sent = sent.reshape(gx_count * gy_count, req_local * MESSAGE, LANES)
     partials = lax.all_to_all(sent, everywhere, split_axis=0, concat_axis=0, tiled=True)
     partials = partials.reshape(gx_count, gy_count, req_local * MESSAGE, LANES)
-    attended = attend(lengths, partials, cosine, sine, kv_cache)
+    cached_keys = jnp.swapaxes(kv_cache[:, :, :HEAD], 1, 2)
+    attended = attend(lengths, partials, cosine, sine, cached_keys, kv_cache)
     attended = attended.reshape(gx_count * gy_count, req_local * REPLY, LANES)
     attended = lax.all_to_all(attended, everywhere, split_axis=0, concat_axis=0, tiled=True)
     attended = attended.reshape(-1, LANES)
 
     shifts = jnp.arange(ring, dtype=jnp.int32)
     ahead = (y + shifts) % ring * 2
-    for_other = output_partial(ahead + 1 - core, attended, out_weight, rows)
+    order = jnp.concatenate([ahead + 1 - core, ahead + core])
+    arranged = arrange(order, attended, rows, out_weight.shape[0])
+    for_other = output_partial(0, arranged, out_weight, rows)
     from_other = move(for_other, 0, 1)
-    mine = output_partial(ahead + core, attended, out_weight, rows)
+    mine = output_partial(1, arranged, out_weight, rows)
     mine = plus(mine, from_other)
     cut = rows // 2
     front = move(mine[2, :cut], 1, 0)
     back = move(mine[2, cut:], -1, 0)
-    up = jnp.concatenate([plus(mine[1, :cut], front), mine[1, cut:]], 0)
-    down = jnp.concatenate([mine[3, :cut], plus(mine[3, cut:], back)], 0)
-    from_below = move(up, 1, 0)
-    from_above = move(down, -1, 0)
-    result = (
-        mine[0].astype(jnp.float32)
-        + from_below.astype(jnp.float32)
-        + from_above.astype(jnp.float32)
-    ).astype(jnp.bfloat16)
+    from_below = move(mine[1], 1, 0)
+    from_above = move(mine[3], -1, 0)
+    far = jnp.concatenate([move(front, 1, 0), move(back, -1, 0)], 0)
+    terms = [mine[0], from_below, from_above, far]
+    result = sum(term.astype(jnp.float32) for term in terms).astype(jnp.bfloat16)
     return result.reshape(steps, block_requests, -1)
 
 

time: 146 us -> 143 us (0.979)
  waiting for transfers between devices: 82.7 us -> 59.4 us
  local copies, waits for them, and re-layouts: 4.35 us -> 21.8 us
  starting transfers between devices: 26.7 us -> 33.9 us
  Pallas kernels: 28.1 us -> 25 us
    all_to_all x1, waiting for transfers between devices: 34.6 us -> 15.5 us  [per_device(): lax.all_to_all(sent, everywhere, split_axis=0, concat_axis=0, tiled=True)]
    unnamed x20 -> x9, local copies, waits for them, and re-layouts: 3.41 us -> 13.7 us
    slice x0 -> x1, local copies, waits for them, and re-layouts: none -> 7.14 us  [per_device(): cached_keys = jnp.swapaxes(kv_cache[:, :, :HEAD], 1, 2)]
    ppermute x13 -> x15, starting transfers between devices: 12.8 us -> 17.5 us  [move(): return lax.ppermute(value, 'gy', across(step_y, step_core))]
    ppermute x13 -> x15, waiting for transfers between devices: 15 us -> 10.9 us  [move(): return lax.ppermute(value, 'gy', across(step_y, step_core))]
    all_to_all x1, starting transfers between devices: 9.13 us -> 11.6 us  [per_device(): lax.all_to_all(sent, everywhere, split_axis=0, concat_axis=0, tiled=True)]
    pallas_call x1, Pallas kernels: 12.1 us -> 10.3 us  [attend(): pl.pallas_call(attend_kernel, out_shape=jax.ShapeDtypeStruct((peers, repl...]
    pallas_call x2 -> x3, Pallas kernels: 5.01 us -> 4.6 us  [the longest x2 3.37 us: output_partial(): pl.pallas_call(functools.partial(output_kernel, half), out_shape=jax.Shap...]
  transfers between devices with their start and end apart: 15 -> 17, of which waited for: 7 -> 6; matrix products, arithmetic and copies ran while one was open for 2% -> 15% of each run, Pallas kernels for 5% -> 5%
where the time goes in v3:
time: 143 us; the launch traced here: 142 us
  waiting for transfers between devices  59.4 us (42%)
  starting transfers between devices  33.9 us (24%)
  Pallas kernels  25 us (17%)
  local copies, waits for them, and re-layouts  21.8 us (15%)
  other arithmetic  2.18 us (2%)
    all_to_all x1, waiting for transfers between devices, per_device(): lax.all_to_all(attended, everywhere, split_axis=0, concat_axis=0, tiled=T...  33 us
    ppermute x15, starting transfers between devices, move(): return lax.ppermute(value, 'gy', across(step_y, step_core))  17.5 us
    all_to_all x1, waiting for transfers between devices, per_device(): lax.all_to_all(sent, everywhere, split_axis=0, concat_axis=0, tiled=True)  15.5 us
    unnamed x9, local copies, waits for them, and re-layouts  13.7 us
    all_to_all x1, starting transfers between devices, per_device(): lax.all_to_all(sent, everywhere, split_axis=0, concat_axis=0, tiled=True)  11.6 us
    ppermute x15, waiting for transfers between devices, move(): return lax.ppermute(value, 'gy', across(step_y, step_core))  10.9 us
    pallas_call x1, Pallas kernels, attend(): pl.pallas_call(attend_kernel, out_shape=jax.ShapeDtypeStruct((peers, repl...  10.3 us
    pallas_call x2, Pallas kernels, project(): pl.pallas_call(functools.partial(project_kernel, count), out_shape=jax.Sh...  10.1 us
  transfers between devices with their start and end apart: 17, of which 6 were waited for; matrix products, arithmetic and copies ran while one was open for 15% of the time, Pallas kernels for 5%

profile of v3, /device:TPU:0, one launch (start us, length us, event | category | flops | bytes accessed | tf_op | source)
XLA Modules:
  0.0 142.5 jit_solution(18247505459006373447)
XLA Ops:
  0.0 0.0 collective-permute-start.6
  0.0 3.2 %collective-permute-start.2 = (bf16[96,1152]{1,0:T(8,128)(2,1)}, bf16[96,1152]{1,0:T(8,128)(2,1)S(1)}, u32[]{:S(2)}, u32[]{:S(2)}) collective-permute-start(bf16[96,1152]{1,0:T(8,128)(2,1)} %bitcast.32), channel_id=1, source_target_pairs={{0,6},{1,7},{2,0},{3,1},{4,2},{5,3},{6,4},{7,5},{8,14},{9,15},{10,... | collective-permute-start | bytes 663560 | tf_op jit(solution)/shard_map/ppermute | solution.py:32
  3.2 0.7 constant_dynamic-slice_fusion.refs_5_
  3.9 4.8 %collective-permute-done.2.refs_3_ = bf16[96,1152]{1,0:T(8,128)(2,1)S(1)} collective-permute-done((bf16[96,1152]{1,0:T(8,128)(2,1)}, bf16[96,1152]{1,0:T(8,128)(2,1)S(1)}, u32[]{:S(2)}, u32[]{:S(2)}) %collective-permute-start.2) | collective-permute-done | bytes 221216 | tf_op jit(solution)/shard_map/ppermute | solution.py:32
  8.8 3.7 %collective-permute-start.5 = (bf16[48,1152]{1,0:T(8,128)(2,1)S(1)}, bf16[48,1152]{1,0:T(8,128)(2,1)S(1)}, u32[]{:S(2)}, u32[]{:S(2)}) collective-permute-start(bf16[48,1152]{1,0:T(8,128)(2,1)S(1)} %slice.33), channel_id=1, source_target_pairs={{0,6},{1,7},{2,0},{3,1},{4,2},{5,3},{6,4},{7,5},{8,14},{9,15},{10,... | collective-permute-start | bytes 331784 | tf_op jit(solution)/shard_map/ppermute | solution.py:32
  12.4 0.0 collective-permute-done.refs_2_
  12.5 0.1 collective-permute-start.4
  12.5 0.1 pad_add_fusion.2.places
  12.6 0.0 collective-permute-start.3
  12.7 0.5 collective-permute-start.1
  13.2 0.9 copy-done.2
  14.1 5.1 %project.2.refs_6_ = bf16[10240,128]{1,0:T(8,128)(2,1)} custom-call(s32[4]{0:T(128)S(1)} %pad_add_fusion.2.places, bf16[96,1152]{1,0:T(8,128)(2,1)S(1)} %bitcast.34, bf16[96,1152]{1,0:T(8,128)(2,1)S(1)} %collective-permute-done.6.refs_1_, bf16[96,1152]{1,0:T(8,128)(2,1)S(1)} %collective-permute-done.refs_2_, ...), custom_call_target="tpu_custom_call" | custom-call | tf_op jit(solution)/shard_map/project/pallas_call | solution.py:115
  19.2 0.0 collective-permute-done.4
  19.2 0.2 collective-permute-start.7
  19.4 0.1 pad_add_fusion.1.places
  19.5 0.0 collective-permute-done.3.refs_1_
  19.5 0.0 collective-permute-done.1.refs_0_
  19.5 1.3 collective-permute-done.7.refs_3_
  20.8 5.1 %project.3 = bf16[10240,128]{1,0:T(8,128)(2,1)} custom-call(s32[4]{0:T(128)S(1)} %pad_add_fusion.1.places, bf16[96,1152]{1,0:T(8,128)(2,1)S(1)} %collective-permute-done.1.refs_0_, bf16[96,1152]{1,0:T(8,128)(2,1)S(1)} %collective-permute-done.3.refs_1_, bf16[96,1152]{1,0:T(8,128)(2,1)S(1)} %pad_maximum_fusion.refs_2_, ...), custom_call_target="tpu_custom_call", output_to_operand_aliasing={{}: (7, {})} | custom-call | tf_op jit(solution)/shard_map/project/pallas_call | solution.py:115
  25.9 0.0 copy-start.3
  25.9 11.6 %all-to-all-start = ((bf16[128,80,128]{2,1,0:T(8,128)(2,1)}), bf16[128,80,128]{2,1,0:T(8,128)(2,1)}, u32[]{:S(2)}, u32[]{:S(2)}) async-start(bf16[128,80,128]{2,1,0:T(8,128)(2,1)} %bitcast.36), calls=%async_computation | async-start | bytes 5242880 | tf_op jit(solution)/shard_map/all_to_all | solution.py:376
  37.5 0.1 add_convert_fusion.1
  37.5 0.1 multiply_sine_fusion
  37.7 7.1 %slice.26 = bf16[2,8192,256]{2,1,0:T(8,128)(2,1)} slice(bf16[2,8192,512]{2,1,0:T(8,128)(2,1)} %cache.1), slice={[0:2], [0:8192], [0:256]} | slice | bytes 16777216 | tf_op jit(solution)/shard_map/slice | solution.py:378
  44.9 12.0 %copy.14 = bf16[2,8192,256]{1,2,0:T(8,128)(2,1)} copy(bf16[2,8192,256]{2,1,0:T(8,128)(2,1)} %slice.26) | data formatting | bytes 16777216
  56.9 0.1 pad.7.clone
  56.9 0.7 maximum_maximum_fusion.1
  57.6 15.5 %all-to-all-done = bf16[128,80,128]{2,1,0:T(8,128)(2,1)} async-done(((bf16[128,80,128]{2,1,0:T(8,128)(2,1)}), bf16[128,80,128]{2,1,0:T(8,128)(2,1)}, u32[]{:S(2)}, u32[]{:S(2)}) %all-to-all-start) | async-done | bytes 2621472 | tf_op jit(solution)/shard_map/all_to_all | solution.py:376
  73.2 10.3 %attend.1 = bf16[16,576,128]{2,1,0:T(8,128)(2,1)} custom-call(s32[2]{0:T(128)} %lengths.1, bf16[16,8,80,128]{3,2,1,0:T(8,128)(2,1)} %bitcast.10.partials, f32[2,24,128]{2,1,0:T(8,128)} %get-tuple-element.16.cosine, f32[2,24,128]{2,1,0:T(8,128)} %get-tuple-element.15.sine, bf16[2,256,8192]{2,1,0:T(8,128)(2,1)} %bitcast.35, bf16[2,8192,512]{2,1,0:T(8,128)(2,1)} %cache.1), custom_call_target="tpu_custom_call" | custom-call | tf_op jit(solution)/shard_map/attend/pallas_call | solution.py:265
  83.4 4.9 %all-to-all-start.1 = ((bf16[128,72,128]{2,1,0:T(8,128)(2,1)}), bf16[128,72,128]{2,1,0:T(8,128)(2,1)S(1)}, u32[]{:S(2)}, u32[]{:S(2)}) async-start(bf16[128,72,128]{2,1,0:T(8,128)(2,1)} %bitcast.37), calls=%async_computation.1 | async-start | bytes 4718592 | tf_op jit(solution)/shard_map/all_to_all | solution.py:381
  88.3 0.1 pad_add_fusion.places
  88.4 33.0 %all-to-all-done.1 = bf16[128,72,128]{2,1,0:T(8,128)(2,1)S(1)} async-done(((bf16[128,72,128]{2,1,0:T(8,128)(2,1)}), bf16[128,72,128]{2,1,0:T(8,128)(2,1)S(1)}, u32[]{:S(2)}, u32[]{:S(2)}) %all-to-all-start.1) | async-done | bytes 2359328 | tf_op jit(solution)/shard_map/all_to_all | solution.py:381
  121.4 1.2 arrange.1.arranged
  122.6 0.8 copy-done.1
  123.4 1.7 %output.3 = bf16[4,96,1152]{2,1,0:T(8,128)(2,1)S(1)} custom-call(bf16[768,1536]{1,0:T(8,128)(2,1)S(1)} %arrange.1.arranged, bf16[1536,1152]{1,0:T(8,128)(2,1)S(1)} %copy-done.1), custom_call_target="tpu_custom_call" | custom-call | tf_op jit(solution)/shard_map/output/pallas_call | solution.py:334
  125.0 0.1 collective-permute-start.8
  125.1 1.7 %output.2 = bf16[4,96,1152]{2,1,0:T(8,128)(2,1)S(1)} custom-call(bf16[768,1536]{1,0:T(8,128)(2,1)S(1)} %arrange.1.arranged, bf16[1536,1152]{1,0:T(8,128)(2,1)S(1)} %copy-done.1), custom_call_target="tpu_custom_call" | custom-call | tf_op jit(solution)/shard_map/output/pallas_call | solution.py:334
  126.8 0.7 collective-permute-done.8
  127.6 0.2 add_convert_fusion
  127.8 0.4 collective-permute-start.11
  128.2 2.9 %collective-permute-start.13 = (bf16[48,1152]{1,0:T(8,128)(2,1)S(1)}, bf16[48,1152]{1,0:T(8,128)(2,1)S(1)}, u32[]{:S(2)}, u32[]{:S(2)}) collective-permute-start(bf16[48,1152]{1,0:T(8,128)(2,1)S(1)} %get-tuple-element.10), channel_id=1, source_target_pairs={{0,6},{1,7},{2,0},{3,1},{4,2},{5,3},{6,4},{7,5},{8,14},{9,15},{10,... | collective-permute-start | bytes 331784 | tf_op jit(solution)/shard_map/ppermute | solution.py:32
  131.1 3.2 %collective-permute-start.10 = (bf16[96,1152]{1,0:T(8,128)(2,1)S(1)}, bf16[96,1152]{1,0:T(8,128)(2,1)S(1)}, u32[]{:S(2)}, u32[]{:S(2)}) collective-permute-start(bf16[96,1152]{1,0:T(8,128)(2,1)S(1)} %get-tuple-element.12), channel_id=1, source_target_pairs={{0,6},{1,7},{2,0},{3,1},{4,2},{5,3},{6,4},{7,5},{8,14},{9,15},{10,... | collective-permute-start | bytes 663560 | tf_op jit(solution)/shard_map/ppermute | solution.py:32
  134.4 0.0 collective-permute-done.11
  134.4 0.0 collective-permute-start.12
  134.4 3.2 %collective-permute-start.14 = (bf16[48,1152]{1,0:T(8,128)(2,1)S(1)}, bf16[48,1152]{1,0:T(8,128)(2,1)S(1)}, u32[]{:S(2)}, u32[]{:S(2)}) collective-permute-start(bf16[48,1152]{1,0:T(8,128)(2,1)S(1)} %collective-permute-done.13), channel_id=1, source_target_pairs={{0,6},{1,7},{2,0},{3,1},{4,2},{5,3},{6,4},{7,5},{8,14},{9,15},{10,... | collective-permute-start | bytes 331784 | tf_op jit(solution)/shard_map/ppermute | solution.py:32
  137.6 4.0 %collective-permute-done.12 = bf16[48,1152]{1,0:T(8,128)(2,1)S(1)} collective-permute-done((bf16[48,1152]{1,0:T(8,128)(2,1)S(1)}, bf16[48,1152]{1,0:T(8,128)(2,1)S(1)}, u32[]{:S(2)}, u32[]{:S(2)}) %collective-permute-start.12) | collective-permute-done | bytes 110624 | tf_op jit(solution)/shard_map/ppermute | solution.py:32
  141.6 0.0 collective-permute-done.14
  141.6 0.8 fusion.2
  (26 shorter events, 0.2 us)
Async XLA Ops:
  0.0 3.2 %copy-start = (bf16[1152,512]{1,0:T(8,128)(2,1)S(1)}, bf16[1152,512]{1,0:T(8,128)(2,1)}, u32[]{:S(2)}) copy-start(bf16[1152,512]{1,0:T(8,128)(2,1)} %param.8) | copy-start | bytes 3538948
  0.0 13.2 %collective-permute-start.6 = (bf16[96,1152]{1,0:T(8,128)(2,1)}, bf16[96,1152]{1,0:T(8,128)(2,1)S(1)}, u32[]{:S(2)}, u32[]{:S(2)}) collective-permute-start(bf16[96,1152]{1,0:T(8,128)(2,1)} %bitcast.31), channel_id=1, source_target_pairs={{0,1},{1,0},{2,3},{3,2},{4,5},{5,4},{6,7},{7,6},{8,9},{9,8},{10,11... | collective-permute-start | bytes 663560 | tf_op jit(solution)/shard_map/ppermute | solution.py:32
  0.0 8.8 %collective-permute-start.2 = (bf16[96,1152]{1,0:T(8,128)(2,1)}, bf16[96,1152]{1,0:T(8,128)(2,1)S(1)}, u32[]{:S(2)}, u32[]{:S(2)}) collective-permute-start(bf16[96,1152]{1,0:T(8,128)(2,1)} %bitcast.32), channel_id=1, source_target_pairs={{0,6},{1,7},{2,0},{3,1},{4,2},{5,3},{6,4},{7,5},{8,14},{9,15},{10,... | collective-permute-start | bytes 663560 | tf_op jit(solution)/shard_map/ppermute | solution.py:32
  3.2 9.3 %collective-permute-start = (bf16[96,1152]{1,0:T(8,128)(2,1)}, bf16[96,1152]{1,0:T(8,128)(2,1)S(1)}, u32[]{:S(2)}, u32[]{:S(2)}) collective-permute-start(bf16[96,1152]{1,0:T(8,128)(2,1)} %bitcast.33), channel_id=1, source_target_pairs={{0,2},{1,3},{2,4},{3,5},{4,6},{5,7},{6,0},{7,1},{8,10},{9,11},{10,... | collective-permute-start | bytes 663560 | tf_op jit(solution)/shard_map/ppermute | solution.py:32
  8.8 10.4 %collective-permute-start.5 = (bf16[48,1152]{1,0:T(8,128)(2,1)S(1)}, bf16[48,1152]{1,0:T(8,128)(2,1)S(1)}, u32[]{:S(2)}, u32[]{:S(2)}) collective-permute-start(bf16[48,1152]{1,0:T(8,128)(2,1)S(1)} %slice.33), channel_id=1, source_target_pairs={{0,6},{1,7},{2,0},{3,1},{4,2},{5,3},{6,4},{7,5},{8,14},{9,15},{10,... | collective-permute-start | bytes 331784 | tf_op jit(solution)/shard_map/ppermute | solution.py:32
  12.5 6.7 %collective-permute-start.4 = (bf16[48,1152]{1,0:T(8,128)(2,1)S(1)}, bf16[48,1152]{1,0:T(8,128)(2,1)S(1)}, u32[]{:S(2)}, u32[]{:S(2)}) collective-permute-start(bf16[48,1152]{1,0:T(8,128)(2,1)S(1)} %slice.32), channel_id=1, source_target_pairs={{0,2},{1,3},{2,4},{3,5},{4,6},{5,7},{6,0},{7,1},{8,10},{9,11},{10,... | collective-permute-start | bytes 331784 | tf_op jit(solution)/shard_map/ppermute | solution.py:32
  12.6 6.9 %collective-permute-start.3 = (bf16[96,1152]{1,0:T(8,128)(2,1)S(1)}, bf16[96,1152]{1,0:T(8,128)(2,1)S(1)}, u32[]{:S(2)}, u32[]{:S(2)}) collective-permute-start(bf16[96,1152]{1,0:T(8,128)(2,1)S(1)} %collective-permute-done.2.refs_3_), channel_id=1, source_target_pairs={{0,1},{1,0},{2,3},{3,2},{4,5},{5,4},{6,7},{7,6},{8,9},{9,8},{10,11... | collective-permute-start | bytes 663560 | tf_op jit(solution)/shard_map/ppermute | solution.py:32
  12.7 6.8 %collective-permute-start.1 = (bf16[96,1152]{1,0:T(8,128)(2,1)S(1)}, bf16[96,1152]{1,0:T(8,128)(2,1)S(1)}, u32[]{:S(2)}, u32[]{:S(2)}) collective-permute-start(bf16[96,1152]{1,0:T(8,128)(2,1)S(1)} %collective-permute-done.refs_2_), channel_id=1, source_target_pairs={{0,1},{1,0},{2,3},{3,2},{4,5},{5,4},{6,7},{7,6},{8,9},{9,8},{10,11... | collective-permute-start | bytes 663560 | tf_op jit(solution)/shard_map/ppermute | solution.py:32
  13.2 0.9 copy-start.2
  19.2 1.6 %collective-permute-start.7 = (bf16[96,1152]{1,0:T(8,128)(2,1)S(1)}, bf16[96,1152]{1,0:T(8,128)(2,1)S(1)}, u32[]{:S(2)}, u32[]{:S(2)}) collective-permute-start(bf16[96,1152]{1,0:T(8,128)(2,1)S(1)} %pad_maximum_fusion.refs_2_), channel_id=1, source_target_pairs={{0,1},{1,0},{2,3},{3,2},{4,5},{5,4},{6,7},{7,6},{8,9},{9,8},{10,11... | collective-permute-start | bytes 663560 | tf_op jit(solution)/shard_map/ppermute | solution.py:32
  25.9 11.6 %copy-start.3 = (s32[2]{0:T(128)S(1)}, s32[2]{0:T(128)}, u32[]{:S(2)}) copy-start(s32[2]{0:T(128)} %lengths.1) | copy-start | bytes 28
  25.9 47.3 %all-to-all-start = ((bf16[128,80,128]{2,1,0:T(8,128)(2,1)}), bf16[128,80,128]{2,1,0:T(8,128)(2,1)}, u32[]{:S(2)}, u32[]{:S(2)}) async-start(bf16[128,80,128]{2,1,0:T(8,128)(2,1)} %bitcast.36), calls=%async_computation | async-start | bytes 5242880 | tf_op jit(solution)/shard_map/all_to_all | solution.py:376
  83.4 37.9 %all-to-all-start.1 = ((bf16[128,72,128]{2,1,0:T(8,128)(2,1)}), bf16[128,72,128]{2,1,0:T(8,128)(2,1)S(1)}, u32[]{:S(2)}, u32[]{:S(2)}) async-start(bf16[128,72,128]{2,1,0:T(8,128)(2,1)} %bitcast.37), calls=%async_computation.1 | async-start | bytes 4718592 | tf_op jit(solution)/shard_map/all_to_all | solution.py:381
  121.4 2.0 %copy-start.1 = (bf16[1536,1152]{1,0:T(8,128)(2,1)S(1)}, bf16[1536,1152]{1,0:T(8,128)(2,1)}, u32[]{:S(2)}) copy-start(bf16[1536,1152]{1,0:T(8,128)(2,1)} %out_weight.3) | copy-start | bytes 10616836
  125.0 2.5 %collective-permute-start.8 = (bf16[4,96,1152]{2,1,0:T(8,128)(2,1)S(1)}, bf16[4,96,1152]{2,1,0:T(8,128)(2,1)S(1)}, u32[]{:S(2)}, u32[]{:S(2)}) collective-permute-start(bf16[4,96,1152]{2,1,0:T(8,128)(2,1)S(1)} %output.3), channel_id=1, source_target_pairs={{0,1},{1,0},{2,3},{3,2},{4,5},{5,4},{6,7},{7,6},{8,9},{9,8},{10,11... | collective-permute-start | bytes 2654216 | tf_op jit(solution)/shard_map/ppermute | solution.py:32
  127.8 6.5 %collective-permute-start.11 = (bf16[48,1152]{1,0:T(8,128)(2,1)S(1)}, bf16[48,1152]{1,0:T(8,128)(2,1)S(1)}, u32[]{:S(2)}, u32[]{:S(2)}) collective-permute-start(bf16[48,1152]{1,0:T(8,128)(2,1)S(1)} %get-tuple-element.9), channel_id=1, source_target_pairs={{0,2},{1,3},{2,4},{3,5},{4,6},{5,7},{6,0},{7,1},{8,10},{9,11},{10,... | collective-permute-start | bytes 331784 | tf_op jit(solution)/shard_map/ppermute | solution.py:32
  128.2 6.2 %collective-permute-start.13 = (bf16[48,1152]{1,0:T(8,128)(2,1)S(1)}, bf16[48,1152]{1,0:T(8,128)(2,1)S(1)}, u32[]{:S(2)}, u32[]{:S(2)}) collective-permute-start(bf16[48,1152]{1,0:T(8,128)(2,1)S(1)} %get-tuple-element.10), channel_id=1, source_target_pairs={{0,6},{1,7},{2,0},{3,1},{4,2},{5,3},{6,4},{7,5},{8,14},{9,15},{10,... | collective-permute-start | bytes 331784 | tf_op jit(solution)/shard_map/ppermute | solution.py:32
  131.1 10.5 %collective-permute-start.9 = (bf16[96,1152]{1,0:T(8,128)(2,1)S(1)}, bf16[96,1152]{1,0:T(8,128)(2,1)S(1)}, u32[]{:S(2)}, u32[]{:S(2)}) collective-permute-start(bf16[96,1152]{1,0:T(8,128)(2,1)S(1)} %get-tuple-element.11), channel_id=1, source_target_pairs={{0,2},{1,3},{2,4},{3,5},{4,6},{5,7},{6,0},{7,1},{8,10},{9,11},{10,... | collective-permute-start | bytes 663560 | tf_op jit(solution)/shard_map/ppermute | solution.py:32
  131.1 10.5 %collective-permute-start.10 = (bf16[96,1152]{1,0:T(8,128)(2,1)S(1)}, bf16[96,1152]{1,0:T(8,128)(2,1)S(1)}, u32[]{:S(2)}, u32[]{:S(2)}) collective-permute-start(bf16[96,1152]{1,0:T(8,128)(2,1)S(1)} %get-tuple-element.12), channel_id=1, source_target_pairs={{0,6},{1,7},{2,0},{3,1},{4,2},{5,3},{6,4},{7,5},{8,14},{9,15},{10,... | collective-permute-start | bytes 663560 | tf_op jit(solution)/shard_map/ppermute | solution.py:32
  134.4 7.2 %collective-permute-start.12 = (bf16[48,1152]{1,0:T(8,128)(2,1)S(1)}, bf16[48,1152]{1,0:T(8,128)(2,1)S(1)}, u32[]{:S(2)}, u32[]{:S(2)}) collective-permute-start(bf16[48,1152]{1,0:T(8,128)(2,1)S(1)} %collective-permute-done.11), channel_id=1, source_target_pairs={{0,2},{1,3},{2,4},{3,5},{4,6},{5,7},{6,0},{7,1},{8,10},{9,11},{10,... | collective-permute-start | bytes 331784 | tf_op jit(solution)/shard_map/ppermute | solution.py:32
  134.4 7.2 %collective-permute-start.14 = (bf16[48,1152]{1,0:T(8,128)(2,1)S(1)}, bf16[48,1152]{1,0:T(8,128)(2,1)S(1)}, u32[]{:S(2)}, u32[]{:S(2)}) collective-permute-start(bf16[48,1152]{1,0:T(8,128)(2,1)S(1)} %collective-permute-done.13), channel_id=1, source_target_pairs={{0,6},{1,7},{2,0},{3,1},{4,2},{5,3},{6,4},{7,5},{8,14},{9,15},{10,... | collective-permute-start | bytes 331784 | tf_op jit(solution)/shard_map/ppermute | solution.py:32

commit v4 on v3

--- a/solution.py
+++ b/solution.py
@@ -129,6 +129,24 @@
     )(*operands)
 
 
+def transpose_kernel(cache, out):
+    out[0] = cache[0].T
+
+
+def transpose_keys(cache):
+    requests, slots, _ = cache.shape
+    rows = 1024
+    return pl.pallas_call(
+        transpose_kernel,
+        grid=(requests, slots // rows),
+        out_shape=jax.ShapeDtypeStruct((requests, HEAD, slots), cache.dtype),
+        in_specs=[pl.BlockSpec((1, rows, HEAD), lambda request, block: (request, block, 0))],
+        out_specs=pl.BlockSpec((1, HEAD, rows), lambda request, block: (request, 0, block)),
+        compiler_params=pltpu.CompilerParams(vmem_limit_bytes=ATTEND_VMEM),
+        name="transpose_keys",
+    )(cache)
+
+
 def attend_kernel(
     lengths, partials, cosine, sine, cached_keys, cache, out, keys, values, summed, query, replies, narrow,
     score, arrived, sent
@@ -375,7 +393,7 @@
     sent = sent.reshape(gx_count * gy_count, req_local * MESSAGE, LANES)
     partials = lax.all_to_all(sent, everywhere, split_axis=0, concat_axis=0, tiled=True)
     partials = partials.reshape(gx_count, gy_count, req_local * MESSAGE, LANES)
-    cached_keys = jnp.swapaxes(kv_cache[:, :, :HEAD], 1, 2)
+    cached_keys = transpose_keys(kv_cache)
     attended = attend(lengths, partials, cosine, sine, cached_keys, kv_cache)
     attended = attended.reshape(gx_count * gy_count, req_local * REPLY, LANES)
     attended = lax.all_to_all(attended, everywhere, split_axis=0, concat_axis=0, tiled=True)

time: 143 us -> 143 us (level)
  local copies, waits for them, and re-layouts: 21.8 us -> 2.64 us
  Pallas kernels: 25 us -> 38.3 us
  waiting for transfers between devices: 59.4 us -> 65.3 us
    pallas_call x0 -> x1, Pallas kernels: none -> 13.2 us  [transpose_keys(): pl.pallas_call(transpose_kernel, grid=(requests, slots // rows), out_shap...]
    unnamed x9 -> x8, local copies, waits for them, and re-layouts: 13.7 us -> 1.71 us
    slice x1 -> x0, local copies, waits for them, and re-layouts: 7.14 us -> none  [per_device(): cached_keys = jnp.swapaxes(kv_cache[:, :, :HEAD], 1, 2)]
    all_to_all x1, waiting for transfers between devices: 15.5 us -> 21.4 us  [per_device(): lax.all_to_all(sent, everywhere, split_axis=0, concat_axis=0, tiled=True)]
  transfers between devices with their start and end apart: 17 -> 17, of which waited for: 6 -> 6; matrix products, arithmetic and copies ran while one was open for 15% -> 1% of each run, Pallas kernels for 5% -> 14%
where the time goes in v4:
time: 143 us
  waiting for transfers between devices  65.3 us (46%)
  Pallas kernels  38.3 us (27%)
  starting transfers between devices  33.8 us (24%)
  local copies, waits for them, and re-layouts  2.64 us (2%)
  other arithmetic  2.16 us (2%)
    all_to_all x1, waiting for transfers between devices, per_device(): lax.all_to_all(attended, everywhere, split_axis=0, concat_axis=0, tiled=T...  33 us
    all_to_all x1, waiting for transfers between devices, per_device(): lax.all_to_all(sent, everywhere, split_axis=0, concat_axis=0, tiled=True)  21.4 us
    ppermute x15, starting transfers between devices, move(): return lax.ppermute(value, 'gy', across(step_y, step_core))  17.4 us
    pallas_call x1, Pallas kernels, transpose_keys(): pl.pallas_call(transpose_kernel, grid=(requests, slots // rows), out_shap...  13.2 us
    all_to_all x1, starting transfers between devices, per_device(): lax.all_to_all(sent, everywhere, split_axis=0, concat_axis=0, tiled=True)  11.6 us
    ppermute x15, waiting for transfers between devices, move(): return lax.ppermute(value, 'gy', across(step_y, step_core))  10.9 us
    pallas_call x1, Pallas kernels, attend(): pl.pallas_call(attend_kernel, out_shape=jax.ShapeDtypeStruct((peers, repl...  10.3 us
    pallas_call x2, Pallas kernels, project(): pl.pallas_call(functools.partial(project_kernel, count), out_shape=jax.Sh...  10.2 us
  transfers between devices with their start and end apart: 17, of which 6 were waited for; matrix products, arithmetic and copies ran while one was open for 1% of the time, Pallas kernels for 14%

profile of v4, /device:TPU:0, one launch (start us, length us, event | category | flops | bytes accessed | tf_op | source)
XLA Modules:
  0.0 142.5 jit_solution(2088107151557019656)
XLA Ops:
  0.0 0.0 collective-permute-start.6
  0.0 3.2 %collective-permute-start.2 = (bf16[96,1152]{1,0:T(8,128)(2,1)}, bf16[96,1152]{1,0:T(8,128)(2,1)S(1)}, u32[]{:S(2)}, u32[]{:S(2)}) collective-permute-start(bf16[96,1152]{1,0:T(8,128)(2,1)} %bitcast.31), channel_id=1, source_target_pairs={{0,6},{1,7},{2,0},{3,1},{4,2},{5,3},{6,4},{7,5},{8,14},{9,15},{10,... | collective-permute-start | bytes 663560 | tf_op jit(solution)/shard_map/ppermute | solution.py:32
  3.2 0.7 constant_dynamic-slice_fusion.refs_5_
  3.9 4.8 %collective-permute-done.2.refs_3_ = bf16[96,1152]{1,0:T(8,128)(2,1)S(1)} collective-permute-done((bf16[96,1152]{1,0:T(8,128)(2,1)}, bf16[96,1152]{1,0:T(8,128)(2,1)S(1)}, u32[]{:S(2)}, u32[]{:S(2)}) %collective-permute-start.2) | collective-permute-done | bytes 221216 | tf_op jit(solution)/shard_map/ppermute | solution.py:32
  8.8 3.7 %collective-permute-start.5 = (bf16[48,1152]{1,0:T(8,128)(2,1)S(1)}, bf16[48,1152]{1,0:T(8,128)(2,1)S(1)}, u32[]{:S(2)}, u32[]{:S(2)}) collective-permute-start(bf16[48,1152]{1,0:T(8,128)(2,1)S(1)} %slice.29), channel_id=1, source_target_pairs={{0,6},{1,7},{2,0},{3,1},{4,2},{5,3},{6,4},{7,5},{8,14},{9,15},{10,... | collective-permute-start | bytes 331784 | tf_op jit(solution)/shard_map/ppermute | solution.py:32
  12.4 0.0 collective-permute-done.refs_2_
  12.5 0.1 collective-permute-start.4
  12.5 0.1 pad_add_fusion.2.places
  12.6 0.0 collective-permute-start.3
  12.7 0.5 collective-permute-start.1
  13.2 0.9 copy-done.2
  14.1 5.1 %project.2.refs_6_ = bf16[10240,128]{1,0:T(8,128)(2,1)} custom-call(s32[4]{0:T(128)S(1)} %pad_add_fusion.2.places, bf16[96,1152]{1,0:T(8,128)(2,1)S(1)} %bitcast.33, bf16[96,1152]{1,0:T(8,128)(2,1)S(1)} %collective-permute-done.6.refs_1_, bf16[96,1152]{1,0:T(8,128)(2,1)S(1)} %collective-permute-done.refs_2_, ...), custom_call_target="tpu_custom_call" | custom-call | tf_op jit(solution)/shard_map/project/pallas_call | solution.py:115
  19.2 0.0 collective-permute-done.5
  19.3 0.0 collective-permute-done.4
  19.3 0.1 collective-permute-start.7
  19.4 0.1 pad_add_fusion.1.places
  19.5 1.3 collective-permute-done.7.refs_3_
  20.8 5.1 %project.3 = bf16[10240,128]{1,0:T(8,128)(2,1)} custom-call(s32[4]{0:T(128)S(1)} %pad_add_fusion.1.places, bf16[96,1152]{1,0:T(8,128)(2,1)S(1)} %collective-permute-done.1.refs_0_, bf16[96,1152]{1,0:T(8,128)(2,1)S(1)} %collective-permute-done.3.refs_1_, bf16[96,1152]{1,0:T(8,128)(2,1)S(1)} %pad_maximum_fusion.refs_2_, ...), custom_call_target="tpu_custom_call", output_to_operand_aliasing={{}: (7, {})} | custom-call | tf_op jit(solution)/shard_map/project/pallas_call | solution.py:115
  25.9 0.0 copy-start.3
  25.9 11.6 %all-to-all-start = ((bf16[128,80,128]{2,1,0:T(8,128)(2,1)}), bf16[128,80,128]{2,1,0:T(8,128)(2,1)}, u32[]{:S(2)}, u32[]{:S(2)}) async-start(bf16[128,80,128]{2,1,0:T(8,128)(2,1)} %bitcast.34), calls=%async_computation | async-start | bytes 5242880 | tf_op jit(solution)/shard_map/all_to_all | solution.py:394
  37.5 0.1 add_convert_fusion.1
  37.6 0.1 multiply_sine_fusion
  37.8 13.2 %transpose_keys.1.cached_keys = bf16[2,256,8192]{2,1,0:T(8,128)(2,1)} custom-call(bf16[2,8192,512]{2,1,0:T(8,128)(2,1)} %cache.3), custom_call_target="tpu_custom_call" | custom-call | tf_op jit(solution)/shard_map/transpose_keys/pallas_call | solution.py:139
  51.0 0.1 pad.7.clone
  51.1 0.7 maximum_maximum_fusion.1
  51.8 21.4 %all-to-all-done = bf16[128,80,128]{2,1,0:T(8,128)(2,1)} async-done(((bf16[128,80,128]{2,1,0:T(8,128)(2,1)}), bf16[128,80,128]{2,1,0:T(8,128)(2,1)}, u32[]{:S(2)}, u32[]{:S(2)}) %all-to-all-start) | async-done | bytes 2621472 | tf_op jit(solution)/shard_map/all_to_all | solution.py:394
  73.2 10.3 %attend.1 = bf16[16,576,128]{2,1,0:T(8,128)(2,1)} custom-call(s32[2]{0:T(128)} %lengths.1, bf16[16,8,80,128]{3,2,1,0:T(8,128)(2,1)} %bitcast.10.partials, f32[2,24,128]{2,1,0:T(8,128)} %get-tuple-element.16.cosine, f32[2,24,128]{2,1,0:T(8,128)} %get-tuple-element.15.sine, bf16[2,256,8192]{2,1,0:T(8,128)(2,1)} %transpose_keys.1.cached_keys, ...), custom_call_target="tpu_custom_call" | custom-call | tf_op jit(solution)/shard_map/attend/pallas_call | solution.py:283
  83.5 4.9 %all-to-all-start.1 = ((bf16[128,72,128]{2,1,0:T(8,128)(2,1)}), bf16[128,72,128]{2,1,0:T(8,128)(2,1)S(1)}, u32[]{:S(2)}, u32[]{:S(2)}) async-start(bf16[128,72,128]{2,1,0:T(8,128)(2,1)} %bitcast.35), calls=%async_computation.1 | async-start | bytes 4718592 | tf_op jit(solution)/shard_map/all_to_all | solution.py:399
  88.4 0.1 pad_add_fusion.places
  88.4 33.0 %all-to-all-done.1 = bf16[128,72,128]{2,1,0:T(8,128)(2,1)S(1)} async-done(((bf16[128,72,128]{2,1,0:T(8,128)(2,1)}), bf16[128,72,128]{2,1,0:T(8,128)(2,1)S(1)}, u32[]{:S(2)}, u32[]{:S(2)}) %all-to-all-start.1) | async-done | bytes 2359328 | tf_op jit(solution)/shard_map/all_to_all | solution.py:399
  121.4 1.2 arrange.1.arranged
  122.6 0.8 copy-done.1
  123.4 1.7 %output.3 = bf16[4,96,1152]{2,1,0:T(8,128)(2,1)S(1)} custom-call(bf16[768,1536]{1,0:T(8,128)(2,1)S(1)} %arrange.1.arranged, bf16[1536,1152]{1,0:T(8,128)(2,1)S(1)} %copy-done.1), custom_call_target="tpu_custom_call" | custom-call | tf_op jit(solution)/shard_map/output/pallas_call | solution.py:352
  125.1 0.1 collective-permute-start.8
  125.2 1.7 %output.2 = bf16[4,96,1152]{2,1,0:T(8,128)(2,1)S(1)} custom-call(bf16[768,1536]{1,0:T(8,128)(2,1)S(1)} %arrange.1.arranged, bf16[1536,1152]{1,0:T(8,128)(2,1)S(1)} %copy-done.1), custom_call_target="tpu_custom_call" | custom-call | tf_op jit(solution)/shard_map/output/pallas_call | solution.py:352
  126.9 0.7 collective-permute-done.8
  127.6 0.2 add_convert_fusion
  127.9 0.4 collective-permute-start.11
  128.3 2.9 %collective-permute-start.13 = (bf16[48,1152]{1,0:T(8,128)(2,1)S(1)}, bf16[48,1152]{1,0:T(8,128)(2,1)S(1)}, u32[]{:S(2)}, u32[]{:S(2)}) collective-permute-start(bf16[48,1152]{1,0:T(8,128)(2,1)S(1)} %get-tuple-element.10), channel_id=1, source_target_pairs={{0,6},{1,7},{2,0},{3,1},{4,2},{5,3},{6,4},{7,5},{8,14},{9,15},{10,... | collective-permute-start | bytes 331784 | tf_op jit(solution)/shard_map/ppermute | solution.py:32
  131.2 0.0 collective-permute-start.9
  131.2 3.2 %collective-permute-start.10 = (bf16[96,1152]{1,0:T(8,128)(2,1)S(1)}, bf16[96,1152]{1,0:T(8,128)(2,1)S(1)}, u32[]{:S(2)}, u32[]{:S(2)}) collective-permute-start(bf16[96,1152]{1,0:T(8,128)(2,1)S(1)} %get-tuple-element.12), channel_id=1, source_target_pairs={{0,6},{1,7},{2,0},{3,1},{4,2},{5,3},{6,4},{7,5},{8,14},{9,15},{10,... | collective-permute-start | bytes 663560 | tf_op jit(solution)/shard_map/ppermute | solution.py:32
  134.4 0.0 collective-permute-done.11
  134.4 0.0 collective-permute-start.12
  134.4 0.0 collective-permute-done.13
  134.4 3.2 %collective-permute-start.14 = (bf16[48,1152]{1,0:T(8,128)(2,1)S(1)}, bf16[48,1152]{1,0:T(8,128)(2,1)S(1)}, u32[]{:S(2)}, u32[]{:S(2)}) collective-permute-start(bf16[48,1152]{1,0:T(8,128)(2,1)S(1)} %collective-permute-done.13), channel_id=1, source_target_pairs={{0,6},{1,7},{2,0},{3,1},{4,2},{5,3},{6,4},{7,5},{8,14},{9,15},{10,... | collective-permute-start | bytes 331784 | tf_op jit(solution)/shard_map/ppermute | solution.py:32
  137.7 4.0 %collective-permute-done.12 = bf16[48,1152]{1,0:T(8,128)(2,1)S(1)} collective-permute-done((bf16[48,1152]{1,0:T(8,128)(2,1)S(1)}, bf16[48,1152]{1,0:T(8,128)(2,1)S(1)}, u32[]{:S(2)}, u32[]{:S(2)}) %collective-permute-start.12) | collective-permute-done | bytes 110624 | tf_op jit(solution)/shard_map/ppermute | solution.py:32
  141.7 0.0 collective-permute-done.14
  141.7 0.8 fusion.2
  (25 shorter events, 0.2 us)
Async XLA Ops:
  0.0 3.2 %copy-start = (bf16[1152,512]{1,0:T(8,128)(2,1)S(1)}, bf16[1152,512]{1,0:T(8,128)(2,1)}, u32[]{:S(2)}) copy-start(bf16[1152,512]{1,0:T(8,128)(2,1)} %param.8) | copy-start | bytes 3538948
  0.0 13.2 %collective-permute-start.6 = (bf16[96,1152]{1,0:T(8,128)(2,1)}, bf16[96,1152]{1,0:T(8,128)(2,1)S(1)}, u32[]{:S(2)}, u32[]{:S(2)}) collective-permute-start(bf16[96,1152]{1,0:T(8,128)(2,1)} %bitcast.30), channel_id=1, source_target_pairs={{0,1},{1,0},{2,3},{3,2},{4,5},{5,4},{6,7},{7,6},{8,9},{9,8},{10,11... | collective-permute-start | bytes 663560 | tf_op jit(solution)/shard_map/ppermute | solution.py:32
  0.0 8.8 %collective-permute-start.2 = (bf16[96,1152]{1,0:T(8,128)(2,1)}, bf16[96,1152]{1,0:T(8,128)(2,1)S(1)}, u32[]{:S(2)}, u32[]{:S(2)}) collective-permute-start(bf16[96,1152]{1,0:T(8,128)(2,1)} %bitcast.31), channel_id=1, source_target_pairs={{0,6},{1,7},{2,0},{3,1},{4,2},{5,3},{6,4},{7,5},{8,14},{9,15},{10,... | collective-permute-start | bytes 663560 | tf_op jit(solution)/shard_map/ppermute | solution.py:32
  3.2 9.3 %collective-permute-start = (bf16[96,1152]{1,0:T(8,128)(2,1)}, bf16[96,1152]{1,0:T(8,128)(2,1)S(1)}, u32[]{:S(2)}, u32[]{:S(2)}) collective-permute-start(bf16[96,1152]{1,0:T(8,128)(2,1)} %bitcast.32), channel_id=1, source_target_pairs={{0,2},{1,3},{2,4},{3,5},{4,6},{5,7},{6,0},{7,1},{8,10},{9,11},{10,... | collective-permute-start | bytes 663560 | tf_op jit(solution)/shard_map/ppermute | solution.py:32
  8.8 10.5 %collective-permute-start.5 = (bf16[48,1152]{1,0:T(8,128)(2,1)S(1)}, bf16[48,1152]{1,0:T(8,128)(2,1)S(1)}, u32[]{:S(2)}, u32[]{:S(2)}) collective-permute-start(bf16[48,1152]{1,0:T(8,128)(2,1)S(1)} %slice.29), channel_id=1, source_target_pairs={{0,6},{1,7},{2,0},{3,1},{4,2},{5,3},{6,4},{7,5},{8,14},{9,15},{10,... | collective-permute-start | bytes 331784 | tf_op jit(solution)/shard_map/ppermute | solution.py:32
  12.5 6.8 %collective-permute-start.4 = (bf16[48,1152]{1,0:T(8,128)(2,1)S(1)}, bf16[48,1152]{1,0:T(8,128)(2,1)S(1)}, u32[]{:S(2)}, u32[]{:S(2)}) collective-permute-start(bf16[48,1152]{1,0:T(8,128)(2,1)S(1)} %slice.28), channel_id=1, source_target_pairs={{0,2},{1,3},{2,4},{3,5},{4,6},{5,7},{6,0},{7,1},{8,10},{9,11},{10,... | collective-permute-start | bytes 331784 | tf_op jit(solution)/shard_map/ppermute | solution.py:32
  12.6 6.9 %collective-permute-start.3 = (bf16[96,1152]{1,0:T(8,128)(2,1)S(1)}, bf16[96,1152]{1,0:T(8,128)(2,1)S(1)}, u32[]{:S(2)}, u32[]{:S(2)}) collective-permute-start(bf16[96,1152]{1,0:T(8,128)(2,1)S(1)} %collective-permute-done.2.refs_3_), channel_id=1, source_target_pairs={{0,1},{1,0},{2,3},{3,2},{4,5},{5,4},{6,7},{7,6},{8,9},{9,8},{10,11... | collective-permute-start | bytes 663560 | tf_op jit(solution)/shard_map/ppermute | solution.py:32
  12.7 6.9 %collective-permute-start.1 = (bf16[96,1152]{1,0:T(8,128)(2,1)S(1)}, bf16[96,1152]{1,0:T(8,128)(2,1)S(1)}, u32[]{:S(2)}, u32[]{:S(2)}) collective-permute-start(bf16[96,1152]{1,0:T(8,128)(2,1)S(1)} %collective-permute-done.refs_2_), channel_id=1, source_target_pairs={{0,1},{1,0},{2,3},{3,2},{4,5},{5,4},{6,7},{7,6},{8,9},{9,8},{10,11... | collective-permute-start | bytes 663560 | tf_op jit(solution)/shard_map/ppermute | solution.py:32
  13.2 0.9 copy-start.2
  19.3 1.6 %collective-permute-start.7 = (bf16[96,1152]{1,0:T(8,128)(2,1)S(1)}, bf16[96,1152]{1,0:T(8,128)(2,1)S(1)}, u32[]{:S(2)}, u32[]{:S(2)}) collective-permute-start(bf16[96,1152]{1,0:T(8,128)(2,1)S(1)} %pad_maximum_fusion.refs_2_), channel_id=1, source_target_pairs={{0,1},{1,0},{2,3},{3,2},{4,5},{5,4},{6,7},{7,6},{8,9},{9,8},{10,11... | collective-permute-start | bytes 663560 | tf_op jit(solution)/shard_map/ppermute | solution.py:32
  25.9 11.6 %copy-start.3 = (s32[2]{0:T(128)S(1)}, s32[2]{0:T(128)}, u32[]{:S(2)}) copy-start(s32[2]{0:T(128)} %lengths.1) | copy-start | bytes 28
  25.9 47.3 %all-to-all-start = ((bf16[128,80,128]{2,1,0:T(8,128)(2,1)}), bf16[128,80,128]{2,1,0:T(8,128)(2,1)}, u32[]{:S(2)}, u32[]{:S(2)}) async-start(bf16[128,80,128]{2,1,0:T(8,128)(2,1)} %bitcast.34), calls=%async_computation | async-start | bytes 5242880 | tf_op jit(solution)/shard_map/all_to_all | solution.py:394
  83.5 37.9 %all-to-all-start.1 = ((bf16[128,72,128]{2,1,0:T(8,128)(2,1)}), bf16[128,72,128]{2,1,0:T(8,128)(2,1)S(1)}, u32[]{:S(2)}, u32[]{:S(2)}) async-start(bf16[128,72,128]{2,1,0:T(8,128)(2,1)} %bitcast.35), calls=%async_computation.1 | async-start | bytes 4718592 | tf_op jit(solution)/shard_map/all_to_all | solution.py:399
  121.4 2.0 %copy-start.1 = (bf16[1536,1152]{1,0:T(8,128)(2,1)S(1)}, bf16[1536,1152]{1,0:T(8,128)(2,1)}, u32[]{:S(2)}) copy-start(bf16[1536,1152]{1,0:T(8,128)(2,1)} %out_weight.3) | copy-start | bytes 10616836
  125.1 2.5 %collective-permute-start.8 = (bf16[4,96,1152]{2,1,0:T(8,128)(2,1)S(1)}, bf16[4,96,1152]{2,1,0:T(8,128)(2,1)S(1)}, u32[]{:S(2)}, u32[]{:S(2)}) collective-permute-start(bf16[4,96,1152]{2,1,0:T(8,128)(2,1)S(1)} %output.3), channel_id=1, source_target_pairs={{0,1},{1,0},{2,3},{3,2},{4,5},{5,4},{6,7},{7,6},{8,9},{9,8},{10,11... | collective-permute-start | bytes 2654216 | tf_op jit(solution)/shard_map/ppermute | solution.py:32
  127.9 6.5 %collective-permute-start.11 = (bf16[48,1152]{1,0:T(8,128)(2,1)S(1)}, bf16[48,1152]{1,0:T(8,128)(2,1)S(1)}, u32[]{:S(2)}, u32[]{:S(2)}) collective-permute-start(bf16[48,1152]{1,0:T(8,128)(2,1)S(1)} %get-tuple-element.9), channel_id=1, source_target_pairs={{0,2},{1,3},{2,4},{3,5},{4,6},{5,7},{6,0},{7,1},{8,10},{9,11},{10,... | collective-permute-start | bytes 331784 | tf_op jit(solution)/shard_map/ppermute | solution.py:32
  128.3 6.2 %collective-permute-start.13 = (bf16[48,1152]{1,0:T(8,128)(2,1)S(1)}, bf16[48,1152]{1,0:T(8,128)(2,1)S(1)}, u32[]{:S(2)}, u32[]{:S(2)}) collective-permute-start(bf16[48,1152]{1,0:T(8,128)(2,1)S(1)} %get-tuple-element.10), channel_id=1, source_target_pairs={{0,6},{1,7},{2,0},{3,1},{4,2},{5,3},{6,4},{7,5},{8,14},{9,15},{10,... | collective-permute-start | bytes 331784 | tf_op jit(solution)/shard_map/ppermute | solution.py:32
  131.2 10.5 %collective-permute-start.9 = (bf16[96,1152]{1,0:T(8,128)(2,1)S(1)}, bf16[96,1152]{1,0:T(8,128)(2,1)S(1)}, u32[]{:S(2)}, u32[]{:S(2)}) collective-permute-start(bf16[96,1152]{1,0:T(8,128)(2,1)S(1)} %get-tuple-element.11), channel_id=1, source_target_pairs={{0,2},{1,3},{2,4},{3,5},{4,6},{5,7},{6,0},{7,1},{8,10},{9,11},{10,... | collective-permute-start | bytes 663560 | tf_op jit(solution)/shard_map/ppermute | solution.py:32
  131.2 10.5 %collective-permute-start.10 = (bf16[96,1152]{1,0:T(8,128)(2,1)S(1)}, bf16[96,1152]{1,0:T(8,128)(2,1)S(1)}, u32[]{:S(2)}, u32[]{:S(2)}) collective-permute-start(bf16[96,1152]{1,0:T(8,128)(2,1)S(1)} %get-tuple-element.12), channel_id=1, source_target_pairs={{0,6},{1,7},{2,0},{3,1},{4,2},{5,3},{6,4},{7,5},{8,14},{9,15},{10,... | collective-permute-start | bytes 663560 | tf_op jit(solution)/shard_map/ppermute | solution.py:32
  134.4 7.2 %collective-permute-start.12 = (bf16[48,1152]{1,0:T(8,128)(2,1)S(1)}, bf16[48,1152]{1,0:T(8,128)(2,1)S(1)}, u32[]{:S(2)}, u32[]{:S(2)}) collective-permute-start(bf16[48,1152]{1,0:T(8,128)(2,1)S(1)} %collective-permute-done.11), channel_id=1, source_target_pairs={{0,2},{1,3},{2,4},{3,5},{4,6},{5,7},{6,0},{7,1},{8,10},{9,11},{10,... | collective-permute-start | bytes 331784 | tf_op jit(solution)/shard_map/ppermute | solution.py:32
  134.4 7.2 %collective-permute-start.14 = (bf16[48,1152]{1,0:T(8,128)(2,1)S(1)}, bf16[48,1152]{1,0:T(8,128)(2,1)S(1)}, u32[]{:S(2)}, u32[]{:S(2)}) collective-permute-start(bf16[48,1152]{1,0:T(8,128)(2,1)S(1)} %collective-permute-done.13), channel_id=1, source_target_pairs={{0,6},{1,7},{2,0},{3,1},{4,2},{5,3},{6,4},{7,5},{8,14},{9,15},{10,... | collective-permute-start | bytes 331784 | tf_op jit(solution)/shard_map/ppermute | solution.py:32
